TPU v7x, 256 devices: a whole 4x4x8 slice. The times are simulated.
256 devices in a mesh: lon: 16 (over y_hi, x, core), lat: 16 (over z, y_lo).
Axes of the slice: x: 4, y: 4 (y_hi: 2, y_lo: 2; y = y_hi * 2 + y_lo), z: 8, core: 2. Of those that a mesh axis runs over, the one named last changes fastest.
Arguments:
- grid_state: bfloat16 [224, 1024, 256], P('lat', 'lon'), may hold values from -6 to 6
- row_query: bfloat16 [256, 256], replicated, may hold values from -15 to 15
- row_keyval: bfloat16 [256, 512], replicated, may hold values from -0.375 to 0.375
- row_output: bfloat16 [256, 256], replicated, may hold values from -0.375 to 0.375
- column_query: bfloat16 [256, 256], replicated, may hold values from -15 to 15
- column_keyval: bfloat16 [256, 512], replicated, may hold values from -0.375 to 0.375
- column_output: bfloat16 [256, 256], replicated, may hold values from -1 to 1
- conv_kernel: float32 [4, 9, 256], replicated, may hold values from -2 to 2
- gate_up: bfloat16 [256, 2048], replicated, may hold values from -0.375 to 0.375
- down_proj: bfloat16 [1024, 256], replicated, may hold values from -0.1875 to 0.1875
Outputs:
- block_out: bfloat16 [224, 1024, 256], P('lat', 'lon')
All inputs are finite; a program needn't handle non-finite values.
Results may differ from a plain program's by a relative error of at most 0.039.
The roundings to bfloat16 on the way count: a program that leaves them out, or rounds other values in their place, can miss the bound.
Values may be sent and summed in bfloat16 or wider, within the bound.
No kernel may reach another device: no remote copies, remote signals or barrier semaphores. Data moves between devices by JAX's collectives and lax.ppermute only.
A program may use at most 128 MiB of HBM per device.

v0:
```python
import functools
import jax
import jax.numpy as jnp
import numpy as np
from jax import lax
from jax.sharding import PartitionSpec as P
from jax.experimental import pallas as pl
from jax.experimental.pallas import tpu as pltpu

BF = jnp.bfloat16
F32 = jnp.float32
HEADS = 8
NT = (((1,), (1,)), ((), ()))
SCALE = 1.4426950408889634 * 32**-0.5
VMEM = pl.BlockSpec(memory_space=pltpu.VMEM)
LIMIT = 56 * 2**20


def norm(values):
    values = values.astype(F32)
    center = values - jnp.mean(values, -1, keepdims=True)
    spread = jnp.mean(center * center, -1, keepdims=True)
    return (center * lax.rsqrt(spread + 1e-5)).astype(BF)


def mm(a, b):
    return jnp.dot(a, b, preferred_element_type=F32)


def value_blocks(values):
    lane = lax.broadcasted_iota(jnp.int32, (1, 128), 1) >> 5
    one = jnp.ones((values.shape[0], 128), BF)
    for h in range(HEADS):
        group = values[:, 128 * (h // 4) : 128 * (h // 4) + 128]
        yield h, jnp.concatenate([jnp.where(lane == h % 4, group, jnp.zeros_like(group)), one], -1)


def attend(q, keys, value_of):
    lane = lax.broadcasted_iota(jnp.int32, (1, 256), 1) >> 5
    halves = []
    for g in range(2):
        total = None
        for h in range(4 * g, 4 * g + 4):
            masked = jnp.where(lane == h, q, jnp.zeros_like(q))
            scores = lax.dot_general(masked, keys, NT, preferred_element_type=F32)
            highest = jnp.max(scores, -1, keepdims=True)
            weights = jnp.exp2((scores - highest) * SCALE).astype(BF)
            sums = mm(weights, value_of(h))
            part = sums[:, :128] / sums[:, 128:]
            total = part if total is None else total + part
        halves.append(total.astype(BF))
    return jnp.concatenate(halves, -1)


def row_kernel(qb, x_ref, wq_ref, wkv_ref, wo_ref, o_ref, q_s, k_s, v_s):
    rows = x_ref.shape[0]
    n = norm(x_ref[...])
    q_s[...] = mm(n, wq_ref[...]).astype(BF)
    kv = mm(n, wkv_ref[...]).astype(BF)
    k_s[...] = kv[:, :256]
    for h, block in value_blocks(kv[:, 256:]):
        v_s[h] = block

    def body(i, _):
        sl = pl.ds(pl.multiple_of(i * qb, qb), qb)
        mixed = attend(q_s[sl, :], k_s[...], lambda h: v_s[h])
        o_ref[sl, :] = (x_ref[sl, :].astype(F32) + mm(mixed, wo_ref[...])).astype(BF)
        return 0

    lax.fori_loop(0, rows // qb, body, 0)


def row_attention(x, wq, wkv, wo, qb=256):
    rows = x.shape[0]
    return pl.pallas_call(
        functools.partial(row_kernel, qb),
        out_shape=jax.ShapeDtypeStruct((rows, 256), BF),
        in_specs=[VMEM] * 4,
        out_specs=VMEM,
        scratch_shapes=[
            pltpu.VMEM((rows, 256), BF),
            pltpu.VMEM((rows, 256), BF),
            pltpu.VMEM((HEADS, rows, 256), BF),
        ],
        compiler_params=pltpu.CompilerParams(vmem_limit_bytes=LIMIT),
        name="row_attention",
    )(x, wq, wkv, wo)


def column_kernel(x_ref, wq_ref, wkv_ref, wo_ref, sel_ref, o_ref):
    lons, lats, _ = x_ref.shape
    peers, _, span, _ = o_ref.shape

    def body(b, _):
        x = x_ref[b]
        n = norm(x)
        q = mm(n, wq_ref[...]).astype(BF)
        kv = mm(n, wkv_ref[...]).astype(BF)
        blocks = dict(value_blocks(kv[:, 256:]))
        mixed = attend(q, kv[:, :256], lambda h: blocks[h])
        after = (x.astype(F32) + mm(mixed, wo_ref[...])).astype(BF)
        sent = mm(sel_ref[...], after).astype(BF)
        for p in range(peers):
            o_ref[p, b] = sent[p * span : (p + 1) * span]
        return 0

    lax.fori_loop(0, lons, body, 0)


def column_attention(x, wq, wkv, wo, select, peers, span):
    lons, lats, _ = x.shape
    return pl.pallas_call(
        column_kernel,
        out_shape=jax.ShapeDtypeStruct((peers, lons, span, 256), BF),
        in_specs=[VMEM] * 5,
        out_specs=VMEM,
        compiler_params=pltpu.CompilerParams(vmem_limit_bytes=LIMIT),
        name="column_attention",
    )(x, wq, wkv, wo, select)


REACH = 15
T, S, PADT = 12, 8, 8
PHI = (
    0.7978842684056429,
    0.036334149112092734,
    -3.302669371540545e-05,
    -5.527338951263253e-05,
    3.974071180846511e-06,
    -1.3378322665984367e-07,
    1.8139279113192596e-09,
)


def gelu(v):
    square = jnp.minimum(v * v, 40.0)
    p = jnp.full_like(square, PHI[-1])
    for c in PHI[-2::-1]:
        p = p * square + c
    half = 0.5 * v
    return half + half * jnp.tanh(v * p)


def conv_mlp_kernel(first_ref, left_ref, own_ref, right_ref, w_ref, gu_ref, down_ref, o_ref, a_s, b_s, f_s):
    per = own_ref.shape[1]
    lat_rows = o_ref.shape[0]
    rows0 = lat_rows + 2 * REACH
    first = first_ref[0]

    def shift(v, by):
        return pltpu.roll(v, by % S, 0)

    def put(ref, hf, row, t, v, reach):
        ref[hf, row, PADT + t] = v
        if t >= T - reach:
            ref[hf, row, PADT + t - T] = shift(v, 1)
        if t < reach:
            ref[hf, row, PADT + t + T] = shift(v, -1)

    parts = [(left_ref, k) for k in range(left_ref.shape[0])]
    parts += [(own_ref, k) for k in range(own_ref.shape[0])]
    parts += [(right_ref, k) for k in range(right_ref.shape[0])]
    for n, (ref, k) in enumerate(parts):
        for b in range(per):
            lon = n * per + b
            s, t = lon // T, lon % T
            for hf in range(2):
                v = ref[k, b, :rows0, hf * 128 : hf * 128 + 128].astype(F32)
                f_s[t, hf, pl.ds(s, rows0, S), :] = v

    def stage(i, _):
        for hf in range(2):
            for t in range(T):
                v = f_s[t, hf, pl.ds(pl.multiple_of(i * S, S), S), :]
                put(a_s, hf, i, t, v, 1)
        return 0

    lax.fori_loop(0, rows0, stage, 0)

    src, dst = a_s, b_s
    edge = 0
    for level in range(4):
        rate = 2**level
        edge += rate
        count = rows0 - 2 * edge
        for hf in range(2):
            taps = [w_ref[level, k, hf] for k in range(9)]

            def row(i, _, src=src, dst=dst, taps=taps, hf=hf, rate=rate, edge=edge, level=level):
                i = i + edge
                lat = first + i
                inside = jnp.logical_and(lat >= 0, lat < LATS).astype(F32)
                for t in range(T):
                    total = None
                    for a in range(3):
                        for b in range(3):
                            term = taps[3 * a + b] * src[hf, i + (a - 1) * rate, PADT + t + (b - 1) * rate]
                            total = term if total is None else total + term
                    new = src[hf, i, PADT + t] + gelu(total)
                    new = new.astype(BF).astype(F32)
                    if level < 3:
                        put(dst, hf, i, t, new * inside, 2 * rate)
                    else:
                        f_s[0, hf, pl.ds((i - edge) * (S * T) + t, S, T), :] = new
                return 0

            lax.fori_loop(0, count, row, 0)
        src, dst = dst, src

    own_cols = o_ref.shape[1]
    batch = 7

    def feed(c, _):
        cells = []
        for d in range(batch):
            at = pl.multiple_of((c * batch + d) * (S * T) + 2 * S, S)
            cells.append(
                jnp.concatenate([f_s[0, hf, pl.ds(at, own_cols), :] for hf in range(2)], -1)
            )
        state = jnp.concatenate(cells, 0)
        normed = norm(state)
        both = mm(normed, gu_ref[...])
        units = gu_ref.shape[1] // 2
        gate, up = both[:, :units], both[:, units:]
        hidden = (gate / (1.0 + jnp.exp(-gate)) * up).astype(BF)
        out = (state + mm(hidden, down_ref[...])).astype(BF)
        o_ref[pl.ds(c * batch, batch)] = out.reshape(batch, own_cols, 256)
        return 0

    lax.fori_loop(0, lat_rows // batch, feed, 0)


LATS = 224


def conv_mlp(first, left, own, right, taps, gate_up, down, lat_rows, own_cols):
    rows0 = lat_rows + 2 * REACH
    return pl.pallas_call(
        conv_mlp_kernel,
        out_shape=jax.ShapeDtypeStruct((lat_rows, own_cols, 256), BF),
        in_specs=[pl.BlockSpec(memory_space=pltpu.SMEM)] + [VMEM] * 6,
        out_specs=VMEM,
        scratch_shapes=[
            pltpu.VMEM((2, rows0, T + 2 * PADT, S, 128), F32),
            pltpu.VMEM((2, rows0, T + 2 * PADT, S, 128), F32),
            pltpu.VMEM((T, 2, max(rows0 * S, lat_rows * S * T), 128), F32),
        ],
        compiler_params=pltpu.CompilerParams(vmem_limit_bytes=LIMIT),
        name="conv_mlp",
    )(first, left, own, right, taps, gate_up, down)


def selection(lats, rows, span):
    blocks = lats // rows
    pick = np.zeros((blocks * span, lats), np.float32)
    for p in range(blocks):
        for r in range(rows + 2 * REACH):
            lat = p * rows - REACH + r
            if 0 <= lat < lats:
                pick[p * span + r, (lat % rows) * blocks + lat // rows] = 1
    return pick.astype(BF)


def on_device(
    grid_state,
    row_query,
    row_keyval,
    row_output,
    column_query,
    column_keyval,
    column_output,
    conv_kernel,
    gate_up,
    down_proj,
):
    rows, cols, width = grid_state.shape
    n = lax.axis_size("lon")
    m = lax.axis_size("lat")
    lons = cols // m
    span = 48
    padded = jnp.pad(grid_state, ((0, n - rows), (0, 0), (0, 0)))
    lines = lax.all_to_all(padded, "lon", 0, 0, tiled=True).reshape(n * cols, width)
    after_rows = row_attention(lines, row_query, row_keyval, row_output)
    moved = lax.all_to_all(after_rows.reshape(n * m, lons, width), ("lon", "lat"), 0, 0, tiled=True)
    moved = jnp.swapaxes(moved[: rows * m], 0, 1)
    pick = jnp.asarray(selection(rows * m, rows, span))
    sent = column_attention(moved, column_query, column_keyval, column_output, pick, m, span)
    own = lax.all_to_all(sent.reshape(m, lons * span, width), "lat", 0, 0, tiled=True)
    own = own.reshape(m, lons, span, width)
    k = 16 // lons
    left = lax.ppermute(own[m - k :], "lon", [(i, (i + 1) % n) for i in range(n)])
    right = lax.ppermute(own[:k], "lon", [((i + 1) % n, i) for i in range(n)])
    first = (lax.axis_index("lat") * rows - REACH).astype(jnp.int32).reshape(1)
    taps = jnp.broadcast_to(conv_kernel.reshape(4, 9, 2, 1, 128), (4, 9, 2, 8, 128))
    return conv_mlp(first, left, own, right, taps, gate_up, down_proj, rows, cols)


def solution(mesh):
    return jax.shard_map(
        on_device,
        mesh=mesh,
        in_specs=(P("lat", "lon", None), P(), P(), P(), P(), P(), P(), P(), P(), P()),
        out_specs=P("lat", "lon", None),
        check_vma=False,
    )
```

profile of v0, /device:TPU:7, one launch (start us, length us, event | category | flops | bytes accessed | tf_op | source)
XLA Modules:
  0.0 162.9 jit_solution(7957658574657168304)
XLA Ops:
  0.0 1.1 pad.4
  1.1 17.6 %all_to_all.15 = bf16[16,64,256]{2,1,0:T(8,128)(2,1)} all-to-all(bf16[16,64,256]{2,1,0:T(8,128)(2,1)S(1)} %pad.4), channel_id=1, replica_groups=mesh['lon'=16,'lat'=16] {'lon'}, dimensions={0} | all-to-all | bytes 1048576 | tf_op jit(solution)/shard_map/all_to_all | solution.py:282
  18.7 14.7 %row_attention.1 = bf16[1024,256]{1,0:T(8,128)(2,1)} custom-call(bf16[1024,256]{1,0:T(8,128)(2,1)} %bitcast.13, bf16[256,256]{1,0:T(8,128)(2,1)} %wq_ref.2, bf16[256,512]{1,0:T(8,128)(2,1)} %wkv_ref.2, bf16[256,256]{1,0:T(8,128)(2,1)} %wo_ref.2), custom_call_target="tpu_custom_call" | custom-call | tf_op jit(solution)/shard_map/row_attention/pallas_call | solution.py:75
  33.4 1.2 reshape.21
  34.6 30.7 %all_to_all.16 = bf16[256,4,256]{2,1,0:T(4,128)(2,1)S(1)} all-to-all(bf16[256,4,256]{2,1,0:T(4,128)(2,1)S(1)} %reshape.21), channel_id=1, replica_groups=mesh['lon'=16,'lat'=16] {'lon','lat'}, dimensions={0} | all-to-all | bytes 1048576 | tf_op jit(solution)/shard_map/all_to_all | solution.py:284
  65.3 0.2 slice.20
  65.5 0.8 copy.19
  66.3 8.7 %column_attention.1 = bf16[16,4,48,256]{3,2,1,0:T(8,128)(2,1)} custom-call(bf16[4,224,256]{2,1,0:T(8,128)(2,1)} %bitcast.14, bf16[256,256]{1,0:T(8,128)(2,1)} %wq_ref.3, bf16[256,512]{1,0:T(8,128)(2,1)} %wkv_ref.3, bf16[256,256]{1,0:T(8,128)(2,1)} %wo_ref.3, bf16[768,224]{1,0:T(8,128)(2,1)} %constant.14.clone.sel_ref), custom_call_target="tpu_custom_call" | custom-call | tf_op jit(solution)/shard_map/column_attention/pallas_call | solution.py:112
  75.0 42.4 %all_to_all.17 = bf16[16,192,256]{2,1,0:T(8,128)(2,1)S(1)} all-to-all(bf16[16,192,256]{2,1,0:T(8,128)(2,1)} %bitcast.12), channel_id=1, replica_groups=mesh['lon'=16,'lat'=16] {'lat'}, dimensions={0} | all-to-all | bytes 3145728 | tf_op jit(solution)/shard_map/all_to_all | solution.py:288
  117.4 0.0 copy-start
  117.4 0.0 copy-start.3
  117.4 0.1 fusion
  117.5 4.7 %collective-permute-start = (bf16[4,4,48,256]{3,2,1,0:T(8,128)(2,1)S(1)}, bf16[4,4,48,256]{3,2,1,0:T(8,128)(2,1)S(1)}, u32[]{:S(2)}, u32[]{:S(2)}) collective-permute-start(bf16[4,4,48,256]{3,2,1,0:T(8,128)(2,1)S(1)} %bitcast.16), channel_id=1, source_target_pairs={{0,16},{16,32},{32,48},{48,64},{64,80},{80,96},{96,112},{112,128},... | collective-permute-start | bytes 1179656 | tf_op jit(solution)/shard_map/ppermute | solution.py:291
  122.2 0.0 collective-permute-start.1
  122.2 0.0 copy-done.3
  122.2 4.7 %collective-permute-done.left_ref = bf16[4,4,48,256]{3,2,1,0:T(8,128)(2,1)S(1)} collective-permute-done((bf16[4,4,48,256]{3,2,1,0:T(8,128)(2,1)S(1)}, bf16[4,4,48,256]{3,2,1,0:T(8,128)(2,1)S(1)}, u32[]{:S(2)}, u32[]{:S(2)}) %collective-permute-start) | collective-permute-done | bytes 393248 | tf_op jit(solution)/shard_map/ppermute | solution.py:291
  126.9 0.0 copy-start.1
  126.9 6.1 %collective-permute-done.1.right_ref = bf16[4,4,48,256]{3,2,1,0:T(8,128)(2,1)S(1)} collective-permute-done((bf16[4,4,48,256]{3,2,1,0:T(8,128)(2,1)S(1)}, bf16[4,4,48,256]{3,2,1,0:T(8,128)(2,1)S(1)}, u32[]{:S(2)}, u32[]{:S(2)}) %collective-permute-start.1) | collective-permute-done | bytes 393248 | tf_op jit(solution)/shard_map/ppermute | solution.py:292
  133.0 0.0 copy-start.2
  133.0 0.8 broadcast_in_dim.8.w_ref
  133.8 0.0 copy-done
  133.8 0.0 copy-done.1
  133.8 0.1 copy-done.2
  133.9 29.0 %conv_mlp.1 = bf16[14,64,256]{2,1,0:T(8,128)(2,1)} custom-call(s32[1]{0:T(128)} %bitcast.first_ref, bf16[4,4,48,256]{3,2,1,0:T(8,128)(2,1)} %copy-done.1, bf16[16,4,48,256]{3,2,1,0:T(8,128)(2,1)} %bitcast.11, bf16[4,4,48,256]{3,2,1,0:T(8,128)(2,1)} %copy-done.2, f32[4,9,2,8,128]{4,3,2,1,0:T(8,128)} %broadcast_in_dim.8.w_ref, bf16[256,2048]{1,0:T(8,128)(2,1)} %gu_ref.1, ...), custom_call_target="tpu_custom_call" | custom-call | tf_op jit(solution)/shard_map/conv_mlp/pallas_call | solution.py:238
  (2 shorter events, 0.0 us)
Async XLA Ops:
  117.4 16.3 %copy-start = (bf16[16,192,256]{2,1,0:T(8,128)(2,1)}, bf16[16,192,256]{2,1,0:T(8,128)(2,1)S(1)}, u32[]{:S(2)}) copy-start(bf16[16,192,256]{2,1,0:T(8,128)(2,1)S(1)} %all_to_all.17) | copy-start | bytes 4718596
  117.4 4.7 %copy-start.3 = (f32[4,9,256]{2,0,1:T(4,128)S(1)}, f32[4,9,256]{2,0,1:T(4,128)}, u32[]{:S(2)}) copy-start(f32[4,9,256]{2,0,1:T(4,128)} %param.18) | copy-start | bytes 110596
  117.5 9.4 %collective-permute-start = (bf16[4,4,48,256]{3,2,1,0:T(8,128)(2,1)S(1)}, bf16[4,4,48,256]{3,2,1,0:T(8,128)(2,1)S(1)}, u32[]{:S(2)}, u32[]{:S(2)}) collective-permute-start(bf16[4,4,48,256]{3,2,1,0:T(8,128)(2,1)S(1)} %bitcast.16), channel_id=1, source_target_pairs={{0,16},{16,32},{32,48},{48,64},{64,80},{80,96},{96,112},{112,128},... | collective-permute-start | bytes 1179656 | tf_op jit(solution)/shard_map/ppermute | solution.py:291
  122.2 10.8 %collective-permute-start.1 = (bf16[4,4,48,256]{3,2,1,0:T(8,128)(2,1)S(1)}, bf16[4,4,48,256]{3,2,1,0:T(8,128)(2,1)S(1)}, u32[]{:S(2)}, u32[]{:S(2)}) collective-permute-start(bf16[4,4,48,256]{3,2,1,0:T(8,128)(2,1)S(1)} %bitcast.15), channel_id=1, source_target_pairs={{16,0},{32,16},{48,32},{64,48},{80,64},{96,80},{112,96},{128,112},... | collective-permute-start | bytes 1179656 | tf_op jit(solution)/shard_map/ppermute | solution.py:292
  126.9 6.9 %copy-start.1 = (bf16[4,4,48,256]{3,2,1,0:T(8,128)(2,1)}, bf16[4,4,48,256]{3,2,1,0:T(8,128)(2,1)S(1)}, u32[]{:S(2)}) copy-start(bf16[4,4,48,256]{3,2,1,0:T(8,128)(2,1)S(1)} %collective-permute-done.left_ref) | copy-start | bytes 1179652
  133.0 0.9 copy-start.2
where the time goes:
time: 163 us
  blocking collectives  90.8 us (56%)
  Pallas kernels  52.5 us (32%)
  waiting for transfers between devices  10.7 us (7%)
  starting transfers between devices  4.68 us (3%)
  local copies, waits for them, and re-layouts  4.18 us (3%)
    all_to_all x1, blocking collectives, on_device(): lax.all_to_all(sent.reshape(m, lons * span, width), 'lat', 0, 0, tiled=True)  42.4 us
    all_to_all x1, blocking collectives, on_device(): lax.all_to_all(after_rows.reshape(n * m, lons, width), ('lon', 'lat'), 0,...  30.7 us
    pallas_call x1, Pallas kernels, conv_mlp(): pl.pallas_call(conv_mlp_kernel, out_shape=jax.ShapeDtypeStruct((lat_rows,...  29 us
    all_to_all x1, blocking collectives, on_device(): lax.all_to_all(padded, 'lon', 0, 0, tiled=True).reshape(n * cols, width)  17.6 us
    pallas_call x1, Pallas kernels, row_attention(): pl.pallas_call(functools.partial(row_kernel, qb), out_shape=jax.ShapeDtyp...  14.7 us
    pallas_call x1, Pallas kernels, column_attention(): pl.pallas_call(column_kernel, out_shape=jax.ShapeDtypeStruct((peers, lons...  8.73 us
    ppermute x1, waiting for transfers between devices, on_device(): right = lax.ppermute(own[:k], 'lon', [((i + 1) % n, i) for i in range(n)])  6.09 us
    ppermute x1, starting transfers between devices, on_device(): lax.ppermute(own[m - k:], 'lon', [(i, (i + 1) % n) for i in range(n)])  4.67 us
  transfers between devices with their start and end apart: 2, of which 2 were waited for; matrix products, arithmetic and copies ran while one was open for 0% of the time, Pallas kernels for 0%

commit v1 on v0

v1 whole, which is shorter than its diff:
```python
import functools
import jax
import jax.numpy as jnp
import numpy as np
from jax import lax
from jax.sharding import PartitionSpec as P
from jax.experimental import pallas as pl
from jax.experimental.pallas import tpu as pltpu

BF = jnp.bfloat16
F32 = jnp.float32
HEADS = 8
NT = (((1,), (1,)), ((), ()))
SCALE = 1.4426950408889634 * 32**-0.5
VMEM = pl.BlockSpec(memory_space=pltpu.VMEM)
LIMIT = 56 * 2**20


def norm(values):
    values = values.astype(F32)
    center = values - jnp.mean(values, -1, keepdims=True)
    spread = jnp.mean(center * center, -1, keepdims=True)
    return (center * lax.rsqrt(spread + 1e-5)).astype(BF)


def mm(a, b):
    return jnp.dot(a, b, preferred_element_type=F32)


def value_blocks(values):
    lane = lax.broadcasted_iota(jnp.int32, (1, 128), 1) >> 5
    one = jnp.ones((values.shape[0], 128), BF)
    for h in range(HEADS):
        group = values[:, 128 * (h // 4) : 128 * (h // 4) + 128]
        yield h, jnp.concatenate([jnp.where(lane == h % 4, group, jnp.zeros_like(group)), one], -1)


def attend(q, keys, value_of):
    lane = lax.broadcasted_iota(jnp.int32, (1, 256), 1) >> 5
    halves = []
    for g in range(2):
        total = None
        for h in range(4 * g, 4 * g + 4):
            masked = jnp.where(lane == h, q, jnp.zeros_like(q))
            scores = lax.dot_general(masked, keys, NT, preferred_element_type=F32)
            highest = jnp.max(scores, -1, keepdims=True)
            weights = jnp.exp2((scores - highest) * SCALE).astype(BF)
            sums = mm(weights, value_of(h))
            part = sums[:, :128] / sums[:, 128:]
            total = part if total is None else total + part
        halves.append(total.astype(BF))
    return jnp.concatenate(halves, -1)


def row_kernel(qb, x_ref, wq_ref, wkv_ref, wo_ref, o_ref, q_s, k_s, v_s, o_s):
    rows = x_ref.shape[0]
    n = norm(x_ref[...])
    q_s[...] = mm(n, wq_ref[...]).astype(BF)
    kv = mm(n, wkv_ref[...]).astype(BF)
    k_s[...] = kv[:, :256]
    for h, block in value_blocks(kv[:, 256:]):
        v_s[h] = block

    def body(i, _):
        sl = pl.ds(pl.multiple_of(i * qb, qb), qb)
        mixed = attend(q_s[sl, :], k_s[...], lambda h: v_s[h])
        after = x_ref[sl, :].astype(F32) + mm(mixed, wo_ref[...])
        for hf in range(2):
            o_s[pl.ds(hf, qb, 2), :] = after[:, hf * 128 : hf * 128 + 128]
        o_ref[pl.ds(pl.multiple_of(i * 2 * qb, 2 * qb), 2 * qb), :] = o_s[...].astype(BF)
        return 0

    lax.fori_loop(0, rows // qb, body, 0)


def row_attention(x, wq, wkv, wo, qb=256):
    rows = x.shape[0]
    return pl.pallas_call(
        functools.partial(row_kernel, qb),
        out_shape=jax.ShapeDtypeStruct((2 * rows, 128), BF),
        in_specs=[VMEM] * 4,
        out_specs=VMEM,
        scratch_shapes=[
            pltpu.VMEM((rows, 256), BF),
            pltpu.VMEM((rows, 256), BF),
            pltpu.VMEM((HEADS, rows, 256), BF),
            pltpu.VMEM((2 * qb, 128), F32),
        ],
        compiler_params=pltpu.CompilerParams(vmem_limit_bytes=LIMIT),
        name="row_attention",
    )(x, wq, wkv, wo)


def column_kernel(lons, x_ref, wq_ref, wkv_ref, wo_ref, sel_ref, o_ref, x_s, o_s):
    x_s[...] = x_ref[...].astype(F32)
    step = 2 * lons
    lats = x_ref.shape[0] // step

    def body(b, _):
        x = jnp.concatenate([x_s[pl.ds(2 * b + hf, lats, step), :] for hf in range(2)], -1)
        n = norm(x)
        q = mm(n, wq_ref[...]).astype(BF)
        kv = mm(n, wkv_ref[...]).astype(BF)
        blocks = dict(value_blocks(kv[:, 256:]))
        mixed = attend(q, kv[:, :256], lambda h: blocks[h])
        after = (x + mm(mixed, wo_ref[...])).astype(BF)
        sent = mm(sel_ref[...], after)
        for hf in range(2):
            o_s[hf, pl.ds(b, sent.shape[0], lons), :] = sent[:, hf * 128 : hf * 128 + 128]
        return 0

    lax.fori_loop(0, lons, body, 0)
    size = o_ref.shape[1]
    for p in range(o_ref.shape[0]):
        o_ref[p] = o_s[p % 2, p // 2 * size : (p // 2 + 1) * size].astype(BF)


def column_attention(x, wq, wkv, wo, select, lons, peers):
    size = select.shape[0] // (peers // 2) * lons
    return pl.pallas_call(
        functools.partial(column_kernel, lons),
        out_shape=jax.ShapeDtypeStruct((peers, size, 128), BF),
        in_specs=[VMEM] * 5,
        out_specs=VMEM,
        scratch_shapes=[
            pltpu.VMEM(x.shape, F32),
            pltpu.VMEM((2, peers // 2 * size, 128), F32),
        ],
        compiler_params=pltpu.CompilerParams(vmem_limit_bytes=LIMIT),
        name="column_attention",
    )(x, wq, wkv, wo, select)


REACH = 15
T, S, PADT = 12, 8, 4
PHI = (
    0.7978842684056429,
    0.036334149112092734,
    -3.302669371540545e-05,
    -5.527338951263253e-05,
    3.974071180846511e-06,
    -1.3378322665984367e-07,
    1.8139279113192596e-09,
)


def gelu(v):
    square = jnp.minimum(v * v, 40.0)
    p = jnp.full_like(square, PHI[-1])
    for c in PHI[-2::-1]:
        p = p * square + c
    half = 0.5 * v
    return half + half * jnp.tanh(v * p)


def conv_kernel_body(lats, at_ref, left_ref, own_ref, right_ref, w_ref, keep_ref, send_ref, f_s, a_s, b_s, n_s):
    rows = keep_ref.shape[0]
    rows0 = 2 * rows + 2 * REACH
    first, half = at_ref[0], at_ref[1]
    size = own_ref.shape[1]
    per = size // rows0
    subs = 0
    for ref in (left_ref, own_ref, right_ref):
        for k in range(ref.shape[0]):
            f_s[subs * size : (subs + 1) * size] = ref[k].astype(F32)
            subs += 1

    def put(ref, row, t, v, reach):
        ref[row, PADT + t] = v
        if t >= T - reach:
            ref[row, PADT + t - T] = pltpu.roll(v, 1, 0)
        if t < reach:
            ref[row, PADT + t + T] = pltpu.roll(v, S - 1, 0)

    def stage(i, _):
        for t in range(T):
            start = t // per * size + i * per + t % per
            put(a_s, i, t, f_s[pl.ds(start, S, T // per * size), :], 1)
        return 0

    lax.fori_loop(0, rows0, stage, 0)

    def taps_of(level):
        out = []
        for k in range(9):
            both = w_ref[level, k : k + 1, :]
            out.append(jnp.broadcast_to(jnp.where(half == 0, both[:, :128], both[:, 128:]), (S, 128)))
        return out

    def inside(i):
        lat = first + i
        return jnp.logical_and(lat >= 0, lat < lats).astype(F32)

    src, dst = a_s, b_s
    edge = 0
    for level in range(3):
        rate = 2**level
        edge += rate
        taps = taps_of(level)

        def row(i, _, src=src, dst=dst, taps=taps, rate=rate, edge=edge, level=level):
            i = i + edge
            valid = inside(i)
            for t in range(T):
                total = None
                for a in range(3):
                    for b in range(3):
                        term = taps[3 * a + b] * src[i + (a - 1) * rate, PADT + t + (b - 1) * rate]
                        total = term if total is None else total + term
                new = (src[i, PADT + t] + gelu(total)).astype(BF).astype(F32) * valid
                if level < 2:
                    put(dst, i, t, new, 2 * rate)
                else:
                    n_s[pl.ds(i * (S * T) + t, S, T), :] = new
            return 0

        lax.fori_loop(0, rows0 - 2 * edge, row, 0)
        src, dst = dst, src

    rate = 8
    taps = taps_of(3)
    cols = keep_ref.shape[1]
    for ref, base in ((send_ref, (1 - half) * rows), (keep_ref, half * rows)):

        def last(i, _, ref=ref, base=base):
            row = base + REACH + i
            out = []
            for q in range(cols // S):
                def cell(a, b, q=q):
                    at = (row + (a - 1) * rate) * (S * T) + 2 * S + q * S + (b - 1) * rate
                    return n_s[pl.ds(pl.multiple_of(at, S), S), :]

                total = None
                for a in range(3):
                    for b in range(3):
                        term = taps[3 * a + b] * cell(a, b)
                        total = term if total is None else total + term
                out.append(cell(1, 1) + gelu(total))
            ref[i] = jnp.concatenate(out, 0).astype(BF)
            return 0

        lax.fori_loop(0, rows, last, 0)


def convolutions(at, left, own, right, taps, lats, rows, cols):
    rows0 = 2 * rows + 2 * REACH
    subs = left.shape[0] + own.shape[0] + right.shape[0]
    shape = jax.ShapeDtypeStruct((rows, cols, 128), BF)
    return pl.pallas_call(
        functools.partial(conv_kernel_body, lats),
        out_shape=(shape, shape),
        in_specs=[pl.BlockSpec(memory_space=pltpu.SMEM)] + [VMEM] * 4,
        out_specs=(VMEM, VMEM),
        scratch_shapes=[
            pltpu.VMEM((subs * own.shape[1], 128), F32),
            pltpu.VMEM((rows0, T + 2 * PADT, S, 128), F32),
            pltpu.VMEM((rows0, T + 2 * PADT, S, 128), F32),
            pltpu.VMEM((rows0 * S * T, 128), F32),
        ],
        compiler_params=pltpu.CompilerParams(vmem_limit_bytes=LIMIT),
        name="convolutions",
    )(at, left, own, right, taps)


def feed_kernel(batch, at_ref, keep_ref, got_ref, gu_ref, down_ref, o_ref):
    rows, cols, _ = keep_ref.shape
    half = at_ref[1]

    def feed(c, _):
        sl = pl.ds(c * batch, batch)
        keep = keep_ref[sl].reshape(batch * cols, 128)
        got = got_ref[sl].reshape(batch * cols, 128)
        state = jnp.concatenate(
            [jnp.where(half == 0, keep, got), jnp.where(half == 0, got, keep)], -1
        ).astype(F32)
        both = mm(norm(state), gu_ref[...])
        units = gu_ref.shape[1] // 2
        gate, up = both[:, :units], both[:, units:]
        hidden = (gate / (1.0 + jnp.exp(-gate)) * up).astype(BF)
        out = (state + mm(hidden, down_ref[...])).astype(BF)
        o_ref[sl] = out.reshape(batch, cols, 256)
        return 0

    lax.fori_loop(0, rows // batch, feed, 0)


def feed_forward(at, keep, got, gate_up, down, batch=7):
    rows, cols, _ = keep.shape
    return pl.pallas_call(
        functools.partial(feed_kernel, batch),
        out_shape=jax.ShapeDtypeStruct((rows, cols, 256), BF),
        in_specs=[pl.BlockSpec(memory_space=pltpu.SMEM)] + [VMEM] * 4,
        out_specs=VMEM,
        compiler_params=pltpu.CompilerParams(vmem_limit_bytes=LIMIT),
        name="feed_forward",
    )(at, keep, got, gate_up, down)


def selection(lats, rows):
    blocks = lats // rows
    span = 2 * rows + 2 * REACH
    pick = np.zeros((blocks // 2 * span, lats), np.float32)
    for p in range(blocks // 2):
        for r in range(span):
            lat = 2 * p * rows - REACH + r
            if 0 <= lat < lats:
                pick[p * span + r, (lat % rows) * blocks + lat // rows] = 1
    return pick.astype(BF)


def on_device(
    grid_state,
    row_query,
    row_keyval,
    row_output,
    column_query,
    column_keyval,
    column_output,
    conv_kernel,
    gate_up,
    down_proj,
):
    rows, cols, width = grid_state.shape
    n = lax.axis_size("lon")
    m = lax.axis_size("lat")
    lons = cols // m
    padded = jnp.pad(grid_state, ((0, n - rows), (0, 0), (0, 0)))
    lines = lax.all_to_all(padded, "lon", 0, 0, tiled=True).reshape(n * cols, width)
    after_rows = row_attention(lines, row_query, row_keyval, row_output)
    moved = lax.all_to_all(after_rows.reshape(n * m, 2 * lons, 128), ("lon", "lat"), 0, 0, tiled=True)
    moved = moved.reshape(-1, 128)[: rows * m * 2 * lons]
    pick = jnp.asarray(selection(rows * m, rows))
    sent = column_attention(moved, column_query, column_keyval, column_output, pick, lons, m)
    own = lax.all_to_all(sent, "lat", 0, 0, tiled=True)
    k = 16 // lons
    left = lax.ppermute(own[m - k :], "lon", [(i, (i + 1) % n) for i in range(n)])
    right = lax.ppermute(own[:k], "lon", [((i + 1) % n, i) for i in range(n)])
    mine = lax.axis_index("lat")
    at = jnp.stack([mine // 2 * (2 * rows) - REACH, mine % 2]).astype(jnp.int32)
    keep, send = convolutions(at, left, own, right, conv_kernel, rows * m, rows, cols)
    got = lax.ppermute(send, "lat", [(i, i ^ 1) for i in range(m)])
    return feed_forward(at, keep, got, gate_up, down_proj)


def solution(mesh):
    return jax.shard_map(
        on_device,
        mesh=mesh,
        in_specs=(P("lat", "lon", None), P(), P(), P(), P(), P(), P(), P(), P(), P()),
        out_specs=P("lat", "lon", None),
        check_vma=False,
    )
```

time: 163 us -> 147 us (0.902)
  blocking collectives: 90.8 us -> 77.8 us
  Pallas kernels: 52.5 us -> 46.9 us
  waiting for transfers between devices: 10.7 us -> 12.9 us
    all_to_all x2, blocking collectives: 73.1 us -> 60.2 us  [the longest x1 30.9 us: on_device(): lax.all_to_all(after_rows.reshape(n * m, 2 * lons, 128), ('lon', 'lat'),...]
    pallas_call x2 -> x3, Pallas kernels: 37.8 us -> 32.1 us  [the longest x1 18.1 us: convolutions(): pl.pallas_call(functools.partial(conv_kernel_body, lats), out_shape=(shap...]
    ppermute x0 -> x1, waiting for transfers between devices: none -> 5.08 us  [on_device(): got = lax.ppermute(send, 'lat', [(i, i ^ 1) for i in range(m)])]
    ppermute x1, waiting for transfers between devices: 4.65 us -> 1.77 us  [on_device(): lax.ppermute(own[m - k:], 'lon', [(i, (i + 1) % n) for i in range(n)])]
  transfers between devices with their start and end apart: 2 -> 3, of which waited for: 2 -> 3; matrix products, arithmetic and copies ran while one was open for 0% -> 1% of each run, Pallas kernels for 0% -> 0%
where the time goes in v1:
time: 147 us
  blocking collectives  77.8 us (53%)
  Pallas kernels  46.9 us (32%)
  waiting for transfers between devices  12.9 us (9%)
  starting transfers between devices  4.36 us (3%)
  local copies, waits for them, and re-layouts  3.93 us (3%)
    all_to_all x1, blocking collectives, on_device(): lax.all_to_all(after_rows.reshape(n * m, 2 * lons, 128), ('lon', 'lat'),...  30.9 us
    all_to_all x1, blocking collectives, on_device(): own = lax.all_to_all(sent, 'lat', 0, 0, tiled=True)  29.3 us
    pallas_call x1, Pallas kernels, convolutions(): pl.pallas_call(functools.partial(conv_kernel_body, lats), out_shape=(shap...  18.1 us
    all_to_all x1, blocking collectives, on_device(): lax.all_to_all(padded, 'lon', 0, 0, tiled=True).reshape(n * cols, width)  17.6 us
    pallas_call x1, Pallas kernels, row_attention(): pl.pallas_call(functools.partial(row_kernel, qb), out_shape=jax.ShapeDtyp...  14.8 us
    pallas_call x1, Pallas kernels, column_attention(): pl.pallas_call(functools.partial(column_kernel, lons), out_shape=jax.Shap...  8.9 us
    ppermute x1, waiting for transfers between devices, on_device(): right = lax.ppermute(own[:k], 'lon', [((i + 1) % n, i) for i in range(n)])  6.09 us
    pallas_call x1, Pallas kernels, feed_forward(): pl.pallas_call(functools.partial(feed_kernel, batch), out_shape=jax.Shape...  5.13 us
  transfers between devices with their start and end apart: 3, of which 3 were waited for; matrix products, arithmetic and copies ran while one was open for 1% of the time, Pallas kernels for 0%

profile of v1, /device:TPU:7, one launch (start us, length us, event | category | flops | bytes accessed | tf_op | source)
XLA Modules:
  0.0 146.6 jit_solution(13990340126584764576)
XLA Ops:
  0.0 1.1 pad.4
  1.1 17.6 %all_to_all.15 = bf16[16,64,256]{2,1,0:T(8,128)(2,1)} all-to-all(bf16[16,64,256]{2,1,0:T(8,128)(2,1)S(1)} %pad.4), channel_id=1, replica_groups=mesh['lon'=16,'lat'=16] {'lon'}, dimensions={0} | all-to-all | bytes 1048576 | tf_op jit(solution)/shard_map/all_to_all | solution.py:328
  18.7 14.8 %row_attention.1 = bf16[2048,128]{1,0:T(8,128)(2,1)} custom-call(bf16[1024,256]{1,0:T(8,128)(2,1)} %bitcast.6, bf16[256,256]{1,0:T(8,128)(2,1)} %wq_ref.2, bf16[256,512]{1,0:T(8,128)(2,1)} %wkv_ref.2, bf16[256,256]{1,0:T(8,128)(2,1)} %wo_ref.2), custom_call_target="tpu_custom_call" | custom-call | tf_op jit(solution)/shard_map/row_attention/pallas_call | solution.py:78
  33.5 30.9 %all_to_all.16 = bf16[256,8,128]{2,1,0:T(8,128)(2,1)S(1)} all-to-all(bf16[256,8,128]{2,1,0:T(8,128)(2,1)} %bitcast.7), channel_id=1, replica_groups=mesh['lon'=16,'lat'=16] {'lon','lat'}, dimensions={0} | all-to-all | bytes 1048576 | tf_op jit(solution)/shard_map/all_to_all | solution.py:330
  64.4 0.8 slice_bitcast_fusion.x_ref
  65.2 8.9 %column_attention.1 = bf16[16,232,128]{2,1,0:T(8,128)(2,1)} custom-call(bf16[1792,128]{1,0:T(8,128)(2,1)} %slice_bitcast_fusion.x_ref, bf16[256,256]{1,0:T(8,128)(2,1)} %wq_ref.3, bf16[256,512]{1,0:T(8,128)(2,1)} %wkv_ref.3, bf16[256,256]{1,0:T(8,128)(2,1)} %wo_ref.3, bf16[464,224]{1,0:T(8,128)(2,1)} %constant.38.clone.sel_ref), custom_call_target="tpu_custom_call" | custom-call | tf_op jit(solution)/shard_map/column_attention/pallas_call | solution.py:120
  74.1 29.3 %all_to_all.17.own_ref = bf16[16,232,128]{2,1,0:T(8,128)(2,1)S(1)} all-to-all(bf16[16,232,128]{2,1,0:T(8,128)(2,1)} %column_attention.1), channel_id=1, replica_groups=mesh['lon'=16,'lat'=16] {'lat'}, dimensions={0} | all-to-all | bytes 1900544 | tf_op jit(solution)/shard_map/all_to_all | solution.py:334
  103.4 0.0 copy-start
  103.4 0.0 copy-start.4
  103.4 4.4 %collective-permute-start = (bf16[4,232,128]{2,1,0:T(8,128)(2,1)S(1)}, bf16[4,232,128]{2,1,0:T(8,128)(2,1)S(1)}, u32[]{:S(2)}, u32[]{:S(2)}) collective-permute-start(bf16[4,232,128]{2,1,0:T(8,128)(2,1)S(1)} %get-tuple-element.10), channel_id=1, source_target_pairs={{0,16},{16,32},{32,48},{48,64},{64,80},{80,96},{96,112},{112,128},... | collective-permute-start | bytes 712712 | tf_op jit(solution)/shard_map/ppermute | solution.py:336
  107.8 0.0 collective-permute-start.1
  107.8 0.0 copy-done.4
  107.8 0.6 copy.12.w_ref
  108.4 0.6 pad_add_fusion.at_ref
  109.1 1.8 %collective-permute-done.left_ref = bf16[4,232,128]{2,1,0:T(8,128)(2,1)S(1)} collective-permute-done((bf16[4,232,128]{2,1,0:T(8,128)(2,1)S(1)}, bf16[4,232,128]{2,1,0:T(8,128)(2,1)S(1)}, u32[]{:S(2)}, u32[]{:S(2)}) %collective-permute-start) | collective-permute-done | bytes 237600 | tf_op jit(solution)/shard_map/ppermute | solution.py:336
  110.8 6.1 %collective-permute-done.1.right_ref = bf16[4,232,128]{2,1,0:T(8,128)(2,1)S(1)} collective-permute-done((bf16[4,232,128]{2,1,0:T(8,128)(2,1)S(1)}, bf16[4,232,128]{2,1,0:T(8,128)(2,1)S(1)}, u32[]{:S(2)}, u32[]{:S(2)}) %collective-permute-start.1) | collective-permute-done | bytes 237600 | tf_op jit(solution)/shard_map/ppermute | solution.py:337
  116.9 0.0 copy-done
  116.9 0.0 copy-done.1
  116.9 0.7 copy-done.2
  117.6 18.1 %convolutions.1 = (bf16[14,64,128]{2,1,0:T(8,128)(2,1)}, bf16[14,64,128]{2,1,0:T(8,128)(2,1)}) custom-call(s32[2]{0:T(128)} %pad_add_fusion.at_ref, bf16[4,232,128]{2,1,0:T(8,128)(2,1)} %copy-done.1, bf16[16,232,128]{2,1,0:T(8,128)(2,1)} %copy-done, bf16[4,232,128]{2,1,0:T(8,128)(2,1)} %copy-done.2, f32[4,9,256]{2,1,0:T(8,128)} %copy.12.w_ref), custom_call_target="tpu_custom_call" | custom-call | tf_op jit(solution)/shard_map/convolutions/pallas_call | solution.py:249
  135.7 0.0 collective-permute-start.2
  135.7 5.1 %collective-permute-done.2.got_ref = bf16[14,64,128]{2,1,0:T(8,128)(2,1)S(1)} collective-permute-done((bf16[14,64,128]{2,1,0:T(8,128)(2,1)}, bf16[14,64,128]{2,1,0:T(8,128)(2,1)S(1)}, u32[]{:S(2)}, u32[]{:S(2)}) %collective-permute-start.2) | collective-permute-done | bytes 229408 | tf_op jit(solution)/shard_map/ppermute | solution.py:341
  140.8 0.7 copy-done.3
  141.5 5.1 %feed_forward.1 = bf16[14,64,256]{2,1,0:T(8,128)(2,1)} custom-call(s32[2]{0:T(128)} %pad_add_fusion.at_ref, bf16[14,64,128]{2,1,0:T(8,128)(2,1)} %get-tuple-element.7.keep_ref, bf16[14,64,128]{2,1,0:T(8,128)(2,1)} %copy-done.3, bf16[256,2048]{1,0:T(8,128)(2,1)} %gu_ref.1, bf16[1024,256]{1,0:T(8,128)(2,1)} %down_ref.1), custom_call_target="tpu_custom_call" | custom-call | tf_op jit(solution)/shard_map/feed_forward/pallas_call | solution.py:289
  (4 shorter events, 0.0 us)
Async XLA Ops:
  103.4 13.6 %copy-start = (bf16[16,232,128]{2,1,0:T(8,128)(2,1)}, bf16[16,232,128]{2,1,0:T(8,128)(2,1)S(1)}, u32[]{:S(2)}) copy-start(bf16[16,232,128]{2,1,0:T(8,128)(2,1)S(1)} %all_to_all.17.own_ref) | copy-start | bytes 2850820
  103.4 4.4 %copy-start.4 = (f32[4,9,256]{2,0,1:T(4,128)S(1)}, f32[4,9,256]{2,0,1:T(4,128)}, u32[]{:S(2)}) copy-start(f32[4,9,256]{2,0,1:T(4,128)} %param.18) | copy-start | bytes 110596
  103.4 7.4 %collective-permute-start = (bf16[4,232,128]{2,1,0:T(8,128)(2,1)S(1)}, bf16[4,232,128]{2,1,0:T(8,128)(2,1)S(1)}, u32[]{:S(2)}, u32[]{:S(2)}) collective-permute-start(bf16[4,232,128]{2,1,0:T(8,128)(2,1)S(1)} %get-tuple-element.10), channel_id=1, source_target_pairs={{0,16},{16,32},{32,48},{48,64},{64,80},{80,96},{96,112},{112,128},... | collective-permute-start | bytes 712712 | tf_op jit(solution)/shard_map/ppermute | solution.py:336
  107.8 9.1 %collective-permute-start.1 = (bf16[4,232,128]{2,1,0:T(8,128)(2,1)S(1)}, bf16[4,232,128]{2,1,0:T(8,128)(2,1)S(1)}, u32[]{:S(2)}, u32[]{:S(2)}) collective-permute-start(bf16[4,232,128]{2,1,0:T(8,128)(2,1)S(1)} %get-tuple-element.9), channel_id=1, source_target_pairs={{16,0},{32,16},{48,32},{64,48},{80,64},{96,80},{112,96},{128,112},... | collective-permute-start | bytes 712712 | tf_op jit(solution)/shard_map/ppermute | solution.py:337
  110.8 6.1 %copy-start.1 = (bf16[4,232,128]{2,1,0:T(8,128)(2,1)}, bf16[4,232,128]{2,1,0:T(8,128)(2,1)S(1)}, u32[]{:S(2)}) copy-start(bf16[4,232,128]{2,1,0:T(8,128)(2,1)S(1)} %collective-permute-done.left_ref) | copy-start | bytes 712708
  116.9 0.7 copy-start.2
  135.7 5.1 %collective-permute-start.2 = (bf16[14,64,128]{2,1,0:T(8,128)(2,1)}, bf16[14,64,128]{2,1,0:T(8,128)(2,1)S(1)}, u32[]{:S(2)}, u32[]{:S(2)}) collective-permute-start(bf16[14,64,128]{2,1,0:T(8,128)(2,1)} %get-tuple-element.8), channel_id=1, source_target_pairs={{0,1},{1,0},{2,3},{3,2},{4,5},{5,4},{6,7},{7,6},{8,9},{9,8},{10,11... | collective-permute-start | bytes 688136 | tf_op jit(solution)/shard_map/ppermute | solution.py:341
  140.8 0.7 copy-start.3

commit v2 on v1

v2 whole, which is shorter than its diff:
```python
import functools
import jax
import jax.numpy as jnp
import numpy as np
from jax import lax
from jax.sharding import PartitionSpec as P
from jax.experimental import pallas as pl
from jax.experimental.pallas import tpu as pltpu

BF = jnp.bfloat16
F32 = jnp.float32
HEADS = 8
NT = (((1,), (1,)), ((), ()))
SCALE = 1.4426950408889634 * 32**-0.5
VMEM = pl.BlockSpec(memory_space=pltpu.VMEM)
LIMIT = 24 * 2**20


def norm(values):
    values = values.astype(F32)
    center = values - jnp.mean(values, -1, keepdims=True)
    spread = jnp.mean(center * center, -1, keepdims=True)
    return (center * lax.rsqrt(spread + 1e-5)).astype(BF)


def mm(a, b):
    return jnp.dot(a, b, preferred_element_type=F32)


def value_blocks(values):
    lane = lax.broadcasted_iota(jnp.int32, (1, 128), 1) >> 5
    one = jnp.ones((values.shape[0], 128), BF)
    for h in range(HEADS):
        group = values[:, 128 * (h // 4) : 128 * (h // 4) + 128]
        yield h, jnp.concatenate([jnp.where(lane == h % 4, group, jnp.zeros_like(group)), one], -1)


def attend(q, keys, value_of):
    lane = lax.broadcasted_iota(jnp.int32, (1, 256), 1) >> 5
    halves = []
    for g in range(2):
        total = None
        for h in range(4 * g, 4 * g + 4):
            masked = jnp.where(lane == h, q, jnp.zeros_like(q))
            scores = lax.dot_general(masked, keys, NT, preferred_element_type=F32)
            highest = jnp.max(scores, -1, keepdims=True)
            weights = jnp.exp2((scores - highest) * SCALE).astype(BF)
            sums = mm(weights, value_of(h))
            part = sums[:, :128] / sums[:, 128:]
            total = part if total is None else total + part
        halves.append(total.astype(BF))
    return jnp.concatenate(halves, -1)


def row_kernel(qb, x_ref, wq_ref, wkv_ref, wo_ref, o_ref, q_s, k_s, v_s, o_s):
    rows = x_ref.shape[0]
    n = norm(x_ref[...])
    q_s[...] = mm(n, wq_ref[...]).astype(BF)
    kv = mm(n, wkv_ref[...]).astype(BF)
    k_s[...] = kv[:, :256]
    for h, block in value_blocks(kv[:, 256:]):
        v_s[h] = block

    def body(i, _):
        sl = pl.ds(pl.multiple_of(i * qb, qb), qb)
        mixed = attend(q_s[sl, :], k_s[...], lambda h: v_s[h])
        after = x_ref[sl, :].astype(F32) + mm(mixed, wo_ref[...])
        for hf in range(2):
            o_s[pl.ds(hf, qb, 2), :] = after[:, hf * 128 : hf * 128 + 128]
        o_ref[pl.ds(pl.multiple_of(i * 2 * qb, 2 * qb), 2 * qb), :] = o_s[...].astype(BF)
        return 0

    lax.fori_loop(0, rows // qb, body, 0)


def row_attention(x, wq, wkv, wo, qb=256):
    rows = x.shape[0]
    return pl.pallas_call(
        functools.partial(row_kernel, qb),
        out_shape=jax.ShapeDtypeStruct((2 * rows, 128), BF),
        in_specs=[VMEM] * 4,
        out_specs=VMEM,
        scratch_shapes=[
            pltpu.VMEM((rows, 256), BF),
            pltpu.VMEM((rows, 256), BF),
            pltpu.VMEM((HEADS, rows, 256), BF),
            pltpu.VMEM((2 * qb, 128), F32),
        ],
        compiler_params=pltpu.CompilerParams(vmem_limit_bytes=LIMIT),
        name="row_attention",
    )(x, wq, wkv, wo)


def column_kernel(lons, span, x_ref, wq_ref, wkv_ref, wo_ref, sel_ref, o_ref, x_s, o_s):
    step = 2 * lons
    lats = sel_ref.shape[1]
    x_s[...] = x_ref[: lats * step].astype(F32)
    size = lons * span
    blocks = o_ref.shape[0] // 2
    pitch = sel_ref.shape[0] // blocks

    def body(b, _):
        x = jnp.concatenate([x_s[pl.ds(2 * b + hf, lats, step), :] for hf in range(2)], -1)
        n = norm(x)
        q = mm(n, wq_ref[...]).astype(BF)
        kv = mm(n, wkv_ref[...]).astype(BF)
        blocks_of = dict(value_blocks(kv[:, 256:]))
        mixed = attend(q, kv[:, :256], lambda h: blocks_of[h])
        after = (x + mm(mixed, wo_ref[...])).astype(BF)
        sent = mm(sel_ref[...], after)
        for p in range(blocks):
            for hf in range(2):
                part = sent[p * pitch : p * pitch + span, hf * 128 : hf * 128 + 128]
                o_s[hf, pl.ds(p * size + b * span, span), :] = part
        return 0

    lax.fori_loop(0, lons, body, 0)
    for p in range(o_ref.shape[0]):
        o_ref[p] = o_s[p % 2, p // 2 * size : (p // 2 + 1) * size].astype(BF)


def column_attention(x, wq, wkv, wo, select, lons, span, peers):
    size = lons * span
    return pl.pallas_call(
        functools.partial(column_kernel, lons, span),
        out_shape=jax.ShapeDtypeStruct((peers, size, 128), BF),
        in_specs=[VMEM] * 5,
        out_specs=VMEM,
        scratch_shapes=[
            pltpu.VMEM((select.shape[1] * 2 * lons, 128), F32),
            pltpu.VMEM((2, peers // 2 * size, 128), F32),
        ],
        compiler_params=pltpu.CompilerParams(vmem_limit_bytes=LIMIT),
        name="column_attention",
    )(x, wq, wkv, wo, select)


REACH = 15
S = 8
HALO = 16


def gelu(v):
    half = 0.5 * v
    return half + half * lax.erf(v * 0.7071067811865476)


def taps_of(w_ref, level, half):
    out = []
    for k in range(9):
        both = w_ref[k, level : level + 1, :]
        out.append(jnp.broadcast_to(jnp.where(half == 0, both[:, :128], both[:, 128:]), (S, 128)))
    return out


def convolved(src, width, taps, i, at, rate):
    def cell(a, b):
        return src[pl.ds((i + (a - 1) * rate) * width + at + (b - 1) * rate, S), :]

    total = None
    for a in range(3):
        for b in range(3):
            term = taps[3 * a + b] * cell(a, b)
            total = term if total is None else total + term
    return (cell(1, 1) + gelu(total)).astype(BF).astype(F32)


def spread(part, buf, width, lon, rows):
    values = part.astype(F32)
    for b in range(part.shape[0] // rows):
        at = 0
        while at < rows:
            place = b * rows + at
            count = min(rows - at, S - place % S)
            buf[pl.ds(at * width + lon + b, count, width), :] = values[place : place + count]
            at += count


def position(rows):
    index = lax.axis_index("lat")
    return lax.shift_right_logical(index, 1) * (2 * rows) - REACH, lax.bitwise_and(index, 1)


def valid(first, i, lats):
    return jnp.logical_and(first + i >= 0, first + i < lats).astype(F32)


INNER = ((17, 25, 33, 41, 49, 57, 65, 71), (19, 27, 35, 43, 51, 59, 67, 69), (23, 31, 39, 47, 55, 63, 65))
OUTER = ((2, 9, 79, 86), (4, 11, 77, 84), (8, 15, 73, 80))


def inner_kernel(lats, rows, own_ref, w_ref, edge_ref, mid_ref, a_s, b_s):
    first, half = position(rows)
    rows0 = edge_ref.shape[1]
    width = own_ref.shape[0] * own_ref.shape[1] // rows0
    per = own_ref.shape[1] // rows0
    for k in range(own_ref.shape[0]):
        spread(own_ref[k], a_s, width, k * per, rows0)

    def raw(i, _):
        ends = [a_s[pl.ds(i * width + c, S), :] for c in (0, width - S)]
        edge_ref[0, i] = jnp.concatenate(ends, 0).astype(BF)
        return 0

    lax.fori_loop(0, rows0, raw, 0)
    src, dst = a_s, b_s
    edge = 0
    for level in range(3):
        rate = 2**level
        edge += rate
        taps = taps_of(w_ref, level, half)

        def row(i, _, src=src, dst=dst, taps=taps, rate=rate, edge=edge, level=level):
            i = i + edge
            mask = valid(first, i, lats)
            out = [convolved(src, width, taps, i, c - HALO, rate) * mask for c in INNER[level]]
            if level < 2:
                for c, v in zip(INNER[level], out):
                    dst[pl.ds(i * width + c - HALO, S), :] = v
                edge_ref[level + 1, i] = jnp.concatenate([out[0], out[-1]], 0).astype(BF)
            else:
                mid_ref[i - edge] = jnp.concatenate(out, 0).astype(BF)
            return 0

        lax.fori_loop(0, rows0 - 2 * edge, row, 0)
        src, dst = dst, src


def inner_levels(own, taps, lats, rows):
    rows0 = 2 * rows + 2 * REACH
    per = own.shape[0] * own.shape[1]
    return pl.pallas_call(
        functools.partial(inner_kernel, lats, rows),
        out_shape=(
            jax.ShapeDtypeStruct((3, rows0, 2 * S, 128), BF),
            jax.ShapeDtypeStruct((rows0 - 14, len(INNER[2]) * S, 128), BF),
        ),
        in_specs=[VMEM] * 2,
        out_specs=(VMEM, VMEM),
        scratch_shapes=[pltpu.VMEM((per, 128), F32)] * 2,
        compiler_params=pltpu.CompilerParams(vmem_limit_bytes=LIMIT),
        cost_estimate=pl.CostEstimate(flops=60000000, bytes_accessed=8000000, transcendentals=1000000),
        name="inner_levels",
    )(own, taps)


def outer_kernel(lats, left_ref, right_ref, edge_ref, mid_ref, w_ref, keep_ref, send_ref, *bufs):
    rows, cols, _ = keep_ref.shape
    first, half = position(rows)
    rows0 = edge_ref.shape[1]
    width = cols + 2 * HALO
    per = left_ref.shape[1] // rows0
    for k in range(left_ref.shape[0]):
        spread(left_ref[k], bufs[0], width, k * per, rows0)
        spread(right_ref[k], bufs[0], width, HALO + cols + k * per, rows0)

    def ends(i, _):
        for level in range(3):
            at = (HALO, HALO + cols - S) if level == 0 else (INNER[level - 1][0], INNER[level - 1][-1])
            both = edge_ref[level, i].astype(F32)
            for e in range(2):
                bufs[level][pl.ds(i * width + at[e], S), :] = both[e * S : e * S + S]
        return 0

    lax.fori_loop(0, rows0, ends, 0)

    def middle(i, _):
        cells = mid_ref[i].astype(F32)
        for g, c in enumerate(INNER[2]):
            bufs[3][pl.ds((i + 7) * width + c, S), :] = cells[g * S : g * S + S]
        return 0

    lax.fori_loop(0, mid_ref.shape[0], middle, 0)
    edge = 0
    for level in range(3):
        rate = 2**level
        edge += rate
        taps = taps_of(w_ref, level, half)

        def row(i, _, taps=taps, rate=rate, edge=edge, level=level):
            i = i + edge
            mask = valid(first, i, lats)
            out = [convolved(bufs[level], width, taps, i, c, rate) * mask for c in OUTER[level]]
            for c, v in zip(OUTER[level], out):
                bufs[level + 1][pl.ds(i * width + c, S), :] = v
            return 0

        lax.fori_loop(0, rows0 - 2 * edge, row, 0)

    taps = taps_of(w_ref, 3, half)
    for ref, base in ((send_ref, (1 - half) * rows), (keep_ref, half * rows)):

        def last(i, _, ref=ref, base=base):
            row = base + REACH + i
            out = [convolved(bufs[3], width, taps, row, HALO + q * S, 8) for q in range(cols // S)]
            ref[i] = jnp.concatenate(out, 0).astype(BF)
            return 0

        lax.fori_loop(0, rows, last, 0)


def outer_levels(left, right, edge, mid, taps, lats, rows, cols):
    rows0 = edge.shape[1]
    shape = jax.ShapeDtypeStruct((rows, cols, 128), BF)
    return pl.pallas_call(
        functools.partial(outer_kernel, lats),
        out_shape=(shape, shape),
        in_specs=[VMEM] * 5,
        out_specs=(VMEM, VMEM),
        scratch_shapes=[pltpu.VMEM((rows0 * (cols + 2 * HALO), 128), F32)] * 4,
        compiler_params=pltpu.CompilerParams(vmem_limit_bytes=LIMIT),
        cost_estimate=pl.CostEstimate(flops=40000000, bytes_accessed=4000000, transcendentals=500000),
        name="outer_levels",
    )(left, right, edge, mid, taps)


def feed_kernel(batch, keep_ref, got_ref, gu_ref, down_ref, o_ref):
    rows, cols, _ = keep_ref.shape
    half = lax.bitwise_and(lax.axis_index("lat"), 1)

    def feed(c, _):
        sl = pl.ds(c * batch, batch)
        keep = keep_ref[sl].reshape(batch * cols, 128)
        got = got_ref[sl].reshape(batch * cols, 128)
        state = jnp.concatenate(
            [jnp.where(half == 0, keep, got), jnp.where(half == 0, got, keep)], -1
        ).astype(F32)
        both = mm(norm(state), gu_ref[...])
        units = gu_ref.shape[1] // 2
        gate, up = both[:, :units], both[:, units:]
        hidden = (gate / (1.0 + jnp.exp(-gate)) * up).astype(BF)
        out = (state + mm(hidden, down_ref[...])).astype(BF)
        o_ref[sl] = out.reshape(batch, cols, 256)
        return 0

    lax.fori_loop(0, rows // batch, feed, 0)


def feed_forward(keep, got, gate_up, down, batch=7):
    rows, cols, _ = keep.shape
    return pl.pallas_call(
        functools.partial(feed_kernel, batch),
        out_shape=jax.ShapeDtypeStruct((rows, cols, 256), BF),
        in_specs=[VMEM] * 4,
        out_specs=VMEM,
        compiler_params=pltpu.CompilerParams(vmem_limit_bytes=LIMIT),
        name="feed_forward",
    )(keep, got, gate_up, down)


def selection(lats, rows):
    blocks = lats // rows
    span = 2 * rows + 2 * REACH
    pitch = -(-span // 16) * 16
    pick = np.zeros((blocks // 2 * pitch, lats), np.float32)
    for p in range(blocks // 2):
        for r in range(span):
            lat = 2 * p * rows - REACH + r
            if 0 <= lat < lats:
                pick[p * pitch + r, (lat % rows) * blocks + lat // rows] = 1
    return pick.astype(BF)


def on_device(
    grid_state,
    row_query,
    row_keyval,
    row_output,
    column_query,
    column_keyval,
    column_output,
    conv_kernel,
    gate_up,
    down_proj,
):
    rows, cols, width = grid_state.shape
    n = lax.axis_size("lon")
    m = lax.axis_size("lat")
    lons = cols // m
    padded = jnp.pad(grid_state, ((0, n - rows), (0, 0), (0, 0)))
    lines = lax.all_to_all(padded, "lon", 0, 0, tiled=True).reshape(n * cols, width)
    after_rows = row_attention(lines, row_query, row_keyval, row_output)
    moved = lax.all_to_all(after_rows.reshape(n * m, 2 * lons, 128), ("lon", "lat"), 0, 0, tiled=True)
    moved = moved.reshape(-1, 128)
    pick = jnp.asarray(selection(rows * m, rows))
    span = 2 * rows + 2 * REACH
    sent = column_attention(moved, column_query, column_keyval, column_output, pick, lons, span, m)
    own = lax.all_to_all(sent, "lat", 0, 0, tiled=True)
    k = HALO // lons
    left = lax.ppermute(own[m - k :], "lon", [(i, (i + 1) % n) for i in range(n)])
    right = lax.ppermute(own[:k], "lon", [((i + 1) % n, i) for i in range(n)])
    taps = jnp.swapaxes(conv_kernel, 0, 1)
    edge, mid = inner_levels(own, taps, rows * m, rows)
    keep, send = outer_levels(left, right, edge, mid, taps, rows * m, rows, cols)
    got = lax.ppermute(send, "lat", [(i, i ^ 1) for i in range(m)])
    return feed_forward(keep, got, gate_up, down_proj)


def solution(mesh):
    return jax.shard_map(
        on_device,
        mesh=mesh,
        in_specs=(P("lat", "lon", None), P(), P(), P(), P(), P(), P(), P(), P(), P()),
        out_specs=P("lat", "lon", None),
        check_vma=False,
    )
```

time: 147 us -> 128 us (0.87)
  Pallas kernels: 46.9 us -> 38.5 us
  waiting for transfers between devices: 12.9 us -> 5.06 us
  local copies, waits for them, and re-layouts: 3.93 us -> 1.15 us
    ppermute x1, waiting for transfers between devices: 6.09 us -> 0.01 us  [on_device(): right = lax.ppermute(own[:k], 'lon', [((i + 1) % n, i) for i in range(n)])]
    pallas_call x2 -> x3, Pallas kernels: 27 us -> 22.1 us  [the longest x1 8.37 us: inner_levels(): pl.pallas_call(functools.partial(inner_kernel, lats, rows), out_shape=(ja...]
    ppermute x1, starting transfers between devices: 0.01 us -> 2.12 us  [on_device(): right = lax.ppermute(own[:k], 'lon', [((i + 1) % n, i) for i in range(n)])]
    pallas_call x1, Pallas kernels: 14.8 us -> 12.8 us  [row_attention(): pl.pallas_call(functools.partial(row_kernel, qb), out_shape=jax.ShapeDtyp...]
    unnamed x11 -> x20, local copies, waits for them, and re-layouts: 2.04 us -> 0.06 us
    ppermute x1, waiting for transfers between devices: 1.77 us -> 0.01 us  [on_device(): lax.ppermute(own[m - k:], 'lon', [(i, (i + 1) % n) for i in range(n)])]
    pallas_call x1, Pallas kernels: 5.13 us -> 3.53 us  [feed_forward(): pl.pallas_call(functools.partial(feed_kernel, batch), out_shape=jax.Shape...]
  transfers between devices with their start and end apart: 3 -> 3, of which waited for: 3 -> 1; matrix products, arithmetic and copies ran while one was open for 1% -> 0% of each run, Pallas kernels for 0% -> 7%
where the time goes in v2:
time: 128 us; the launch traced here: 127 us
  blocking collectives  77.1 us (60%)
  Pallas kernels  38.5 us (30%)
  starting transfers between devices  5.6 us (4%)
  waiting for transfers between devices  5.06 us (4%)
    all_to_all x1, blocking collectives, on_device(): lax.all_to_all(after_rows.reshape(n * m, 2 * lons, 128), ('lon', 'lat'),...  30.7 us
    all_to_all x1, blocking collectives, on_device(): own = lax.all_to_all(sent, 'lat', 0, 0, tiled=True)  28.7 us
    all_to_all x1, blocking collectives, on_device(): lax.all_to_all(padded, 'lon', 0, 0, tiled=True).reshape(n * cols, width)  17.7 us
    pallas_call x1, Pallas kernels, row_attention(): pl.pallas_call(functools.partial(row_kernel, qb), out_shape=jax.ShapeDtyp...  12.8 us
    pallas_call x1, Pallas kernels, inner_levels(): pl.pallas_call(functools.partial(inner_kernel, lats, rows), out_shape=(ja...  8.37 us
    pallas_call x1, Pallas kernels, outer_levels(): pl.pallas_call(functools.partial(outer_kernel, lats), out_shape=(shape, s...  7.49 us
    pallas_call x1, Pallas kernels, column_attention(): pl.pallas_call(functools.partial(column_kernel, lons, span), out_shape=ja...  6.25 us
    ppermute x1, waiting for transfers between devices, on_device(): got = lax.ppermute(send, 'lat', [(i, i ^ 1) for i in range(m)])  5.05 us
  transfers between devices with their start and end apart: 3, of which 1 were waited for; matrix products, arithmetic and copies ran while one was open for 0% of the time, Pallas kernels for 7%

profile of v2, /device:TPU:7, one launch (start us, length us, event | category | flops | bytes accessed | tf_op | source)
XLA Modules:
  0.0 127.5 jit_solution(4035553357443586859)
XLA Ops:
  0.0 1.1 pad.4
  1.1 0.0 copy-start.4
  1.1 0.0 copy-start.5
  1.1 0.0 copy-start.6
  1.1 17.7 %all_to_all.15 = bf16[16,64,256]{2,1,0:T(8,128)(2,1)S(1)} all-to-all(bf16[16,64,256]{2,1,0:T(8,128)(2,1)S(1)} %pad.4), channel_id=1, replica_groups=mesh['lon'=16,'lat'=16] {'lon'}, dimensions={0} | all-to-all | bytes 1048576 | tf_op jit(solution)/shard_map/all_to_all | solution.py:381
  18.8 12.8 %row_attention.1 = bf16[2048,128]{1,0:T(8,128)(2,1)S(1)} custom-call(bf16[1024,256]{1,0:T(8,128)(2,1)S(1)} %bitcast.5, bf16[256,256]{1,0:T(8,128)(2,1)S(1)} %copy-done.5, bf16[256,512]{1,0:T(8,128)(2,1)S(1)} %copy-done.4, bf16[256,256]{1,0:T(8,128)(2,1)S(1)} %copy-done.6), custom_call_target="tpu_custom_call" | custom-call | tf_op jit(solution)/shard_map/row_attention/pallas_call | solution.py:78
  31.6 0.0 copy-start.2
  31.6 0.0 copy-start.3
  31.6 0.0 copy-start.7
  31.6 0.0 copy-start.8
  31.6 30.7 %all_to_all.16 = bf16[256,8,128]{2,1,0:T(8,128)(2,1)S(1)} all-to-all(bf16[256,8,128]{2,1,0:T(8,128)(2,1)S(1)} %bitcast.6), channel_id=1, replica_groups=mesh['lon'=16,'lat'=16] {'lon','lat'}, dimensions={0} | all-to-all | bytes 1048576 | tf_op jit(solution)/shard_map/all_to_all | solution.py:383
  62.4 6.3 %column_attention.1 = bf16[16,232,128]{2,1,0:T(8,128)(2,1)S(1)} custom-call(bf16[2048,128]{1,0:T(8,128)(2,1)S(1)} %bitcast.4, bf16[256,256]{1,0:T(8,128)(2,1)S(1)} %copy-done.7, bf16[256,512]{1,0:T(8,128)(2,1)S(1)} %copy-done.2, bf16[256,256]{1,0:T(8,128)(2,1)S(1)} %copy-done.8, bf16[512,224]{1,0:T(8,128)(2,1)S(1)} %copy-done.3), custom_call_target="tpu_custom_call" | custom-call | tf_op jit(solution)/shard_map/column_attention/pallas_call | solution.py:124
  68.6 28.7 %all_to_all.17.own_ref = bf16[16,232,128]{2,1,0:T(8,128)(2,1)S(1)} all-to-all(bf16[16,232,128]{2,1,0:T(8,128)(2,1)S(1)} %column_attention.1), channel_id=1, replica_groups=mesh['lon'=16,'lat'=16] {'lat'}, dimensions={0} | all-to-all | bytes 1900544 | tf_op jit(solution)/shard_map/all_to_all | solution.py:388
  97.4 2.1 %collective-permute-start.1 = (bf16[4,232,128]{2,1,0:T(8,128)(2,1)S(1)}, bf16[4,232,128]{2,1,0:T(8,128)(2,1)S(1)}, u32[]{:S(2)}, u32[]{:S(2)}) collective-permute-start(bf16[4,232,128]{2,1,0:T(8,128)(2,1)S(1)} %get-tuple-element.13), channel_id=1, source_target_pairs={{16,0},{32,16},{48,32},{64,48},{80,64},{96,80},{112,96},{128,112},... | collective-permute-start | bytes 712712 | tf_op jit(solution)/shard_map/ppermute | solution.py:391
  99.5 3.3 %collective-permute-start = (bf16[4,232,128]{2,1,0:T(8,128)(2,1)S(1)}, bf16[4,232,128]{2,1,0:T(8,128)(2,1)S(1)}, u32[]{:S(2)}, u32[]{:S(2)}) collective-permute-start(bf16[4,232,128]{2,1,0:T(8,128)(2,1)S(1)} %get-tuple-element.14), channel_id=1, source_target_pairs={{0,16},{16,32},{32,48},{48,64},{64,80},{80,96},{96,112},{112,128},... | collective-permute-start | bytes 712712 | tf_op jit(solution)/shard_map/ppermute | solution.py:390
  102.8 8.4 %inner_levels.1 = (bf16[3,58,16,128]{3,2,1,0:T(8,128)(2,1)S(1)}, bf16[44,56,128]{2,1,0:T(8,128)(2,1)S(1)}) custom-call(bf16[16,232,128]{2,1,0:T(8,128)(2,1)S(1)} %all_to_all.17.own_ref, f32[9,4,256]{2,1,0:T(4,128)S(1)} %bitcast.7), custom_call_target="tpu_custom_call" | custom-call | flops 60000000 | bytes 8000000 | tf_op jit(solution)/shard_map/inner_levels/pallas_call | solution.py:232
  111.2 0.0 copy-start
  111.2 0.0 collective-permute-done.1.right_ref
  111.2 0.0 collective-permute-done.left_ref
  111.2 0.0 copy-start.1
  111.2 7.5 %outer_levels.1 = (bf16[14,64,128]{2,1,0:T(8,128)(2,1)S(1)}, bf16[14,64,128]{2,1,0:T(8,128)(2,1)S(1)}) custom-call(bf16[4,232,128]{2,1,0:T(8,128)(2,1)S(1)} %collective-permute-done.left_ref, bf16[4,232,128]{2,1,0:T(8,128)(2,1)S(1)} %collective-permute-done.1.right_ref, bf16[3,58,16,128]{3,2,1,0:T(8,128)(2,1)S(1)} %get-tuple-element.9.edge_ref, ...), custom_call_target="tpu_custom_call" | custom-call | flops 40000000 | bytes 4000000 | tf_op jit(solution)/shard_map/outer_levels/pallas_call | solution.py:305
  118.7 0.2 collective-permute-start.2
  118.9 5.0 %collective-permute-done.2.got_ref = bf16[14,64,128]{2,1,0:T(8,128)(2,1)S(1)} collective-permute-done((bf16[14,64,128]{2,1,0:T(8,128)(2,1)S(1)}, bf16[14,64,128]{2,1,0:T(8,128)(2,1)S(1)}, u32[]{:S(2)}, u32[]{:S(2)}) %collective-permute-start.2) | collective-permute-done | bytes 229408 | tf_op jit(solution)/shard_map/ppermute | solution.py:395
  124.0 3.5 %feed_forward.1 = bf16[14,64,256]{2,1,0:T(8,128)(2,1)} custom-call(bf16[14,64,128]{2,1,0:T(8,128)(2,1)S(1)} %get-tuple-element.11.keep_ref, bf16[14,64,128]{2,1,0:T(8,128)(2,1)S(1)} %collective-permute-done.2.got_ref, bf16[256,2048]{1,0:T(8,128)(2,1)S(1)} %copy-done, bf16[1024,256]{1,0:T(8,128)(2,1)S(1)} %copy-done.1), custom_call_target="tpu_custom_call" | custom-call | tf_op jit(solution)/shard_map/feed_forward/pallas_call | solution.py:341
  (12 shorter events, 0.1 us)
Async XLA Ops:
  1.1 17.7 %copy-start.4 = (bf16[256,512]{1,0:T(8,128)(2,1)S(1)}, bf16[256,512]{1,0:T(8,128)(2,1)}, u32[]{:S(2)}) copy-start(bf16[256,512]{1,0:T(8,128)(2,1)} %wkv_ref.2) | copy-start | bytes 786436
  1.1 17.7 %copy-start.5 = (bf16[256,256]{1,0:T(8,128)(2,1)S(1)}, bf16[256,256]{1,0:T(8,128)(2,1)}, u32[]{:S(2)}) copy-start(bf16[256,256]{1,0:T(8,128)(2,1)} %wq_ref.2) | copy-start | bytes 393220
  1.1 17.7 %copy-start.6 = (bf16[256,256]{1,0:T(8,128)(2,1)S(1)}, bf16[256,256]{1,0:T(8,128)(2,1)}, u32[]{:S(2)}) copy-start(bf16[256,256]{1,0:T(8,128)(2,1)} %wo_ref.2) | copy-start | bytes 393220
  31.6 30.8 %copy-start.2 = (bf16[256,512]{1,0:T(8,128)(2,1)S(1)}, bf16[256,512]{1,0:T(8,128)(2,1)}, u32[]{:S(2)}) copy-start(bf16[256,512]{1,0:T(8,128)(2,1)} %wkv_ref.3) | copy-start | bytes 786436
  31.6 30.8 %copy-start.3 = (bf16[512,224]{1,0:T(8,128)(2,1)S(1)}, bf16[512,224]{1,0:T(8,128)(2,1)}, u32[]{:S(2)}) copy-start(bf16[512,224]{1,0:T(8,128)(2,1)} %constant.5.clone.sel_ref) | copy-start | bytes 688132
  31.6 30.7 %copy-start.7 = (bf16[256,256]{1,0:T(8,128)(2,1)S(1)}, bf16[256,256]{1,0:T(8,128)(2,1)}, u32[]{:S(2)}) copy-start(bf16[256,256]{1,0:T(8,128)(2,1)} %wq_ref.3) | copy-start | bytes 393220
  31.6 30.7 %copy-start.8 = (bf16[256,256]{1,0:T(8,128)(2,1)S(1)}, bf16[256,256]{1,0:T(8,128)(2,1)}, u32[]{:S(2)}) copy-start(bf16[256,256]{1,0:T(8,128)(2,1)} %wo_ref.3) | copy-start | bytes 393220
  97.3 5.5 %copy-start.9 = (f32[4,9,256]{2,0,1:T(4,128)S(1)}, f32[4,9,256]{2,0,1:T(4,128)}, u32[]{:S(2)}) copy-start(f32[4,9,256]{2,0,1:T(4,128)} %param.18) | copy-start | bytes 110596
  97.4 13.8 %collective-permute-start.1 = (bf16[4,232,128]{2,1,0:T(8,128)(2,1)S(1)}, bf16[4,232,128]{2,1,0:T(8,128)(2,1)S(1)}, u32[]{:S(2)}, u32[]{:S(2)}) collective-permute-start(bf16[4,232,128]{2,1,0:T(8,128)(2,1)S(1)} %get-tuple-element.13), channel_id=1, source_target_pairs={{16,0},{32,16},{48,32},{64,48},{80,64},{96,80},{112,96},{128,112},... | collective-permute-start | bytes 712712 | tf_op jit(solution)/shard_map/ppermute | solution.py:391
  99.5 11.7 %collective-permute-start = (bf16[4,232,128]{2,1,0:T(8,128)(2,1)S(1)}, bf16[4,232,128]{2,1,0:T(8,128)(2,1)S(1)}, u32[]{:S(2)}, u32[]{:S(2)}) collective-permute-start(bf16[4,232,128]{2,1,0:T(8,128)(2,1)S(1)} %get-tuple-element.14), channel_id=1, source_target_pairs={{0,16},{16,32},{32,48},{48,64},{64,80},{80,96},{96,112},{112,128},... | collective-permute-start | bytes 712712 | tf_op jit(solution)/shard_map/ppermute | solution.py:390
  111.2 12.8 %copy-start = (bf16[256,2048]{1,0:T(8,128)(2,1)S(1)}, bf16[256,2048]{1,0:T(8,128)(2,1)}, u32[]{:S(2)}) copy-start(bf16[256,2048]{1,0:T(8,128)(2,1)} %gu_ref.1) | copy-start | bytes 3145732
  111.2 12.7 %copy-start.1 = (bf16[1024,256]{1,0:T(8,128)(2,1)S(1)}, bf16[1024,256]{1,0:T(8,128)(2,1)}, u32[]{:S(2)}) copy-start(bf16[1024,256]{1,0:T(8,128)(2,1)} %down_ref.1) | copy-start | bytes 1572868
  118.7 5.2 %collective-permute-start.2 = (bf16[14,64,128]{2,1,0:T(8,128)(2,1)S(1)}, bf16[14,64,128]{2,1,0:T(8,128)(2,1)S(1)}, u32[]{:S(2)}, u32[]{:S(2)}) collective-permute-start(bf16[14,64,128]{2,1,0:T(8,128)(2,1)S(1)} %get-tuple-element.12), channel_id=1, source_target_pairs={{0,1},{1,0},{2,3},{3,2},{4,5},{5,4},{6,7},{7,6},{8,9},{9,8},{10,11... | collective-permute-start | bytes 688136 | tf_op jit(solution)/shard_map/ppermute | solution.py:395

commit v3 on v2

--- a/solution.py
+++ b/solution.py
@@ -37,12 +37,19 @@
 
 def attend(q, keys, value_of):
     lane = lax.broadcasted_iota(jnp.int32, (1, 256), 1) >> 5
+
+    def scores_of(h):
+        masked = jnp.where(lane == h, q, jnp.zeros_like(q))
+        return lax.dot_general(masked, keys, NT, preferred_element_type=F32)
+
     halves = []
+    later = scores_of(0)
     for g in range(2):
         total = None
         for h in range(4 * g, 4 * g + 4):
-            masked = jnp.where(lane == h, q, jnp.zeros_like(q))
-            scores = lax.dot_general(masked, keys, NT, preferred_element_type=F32)
+            scores = later
+            if h + 1 < HEADS:
+                later = scores_of(h + 1)
             highest = jnp.max(scores, -1, keepdims=True)
             weights = jnp.exp2((scores - highest) * SCALE).astype(BF)
             sums = mm(weights, value_of(h))
@@ -73,7 +80,7 @@
     lax.fori_loop(0, rows // qb, body, 0)
 
 
-def row_attention(x, wq, wkv, wo, qb=256):
+def row_attention(x, wq, wkv, wo, qb=512):
     rows = x.shape[0]
     return pl.pallas_call(
         functools.partial(row_kernel, qb),
@@ -91,7 +98,7 @@
     )(x, wq, wkv, wo)
 
 
-def column_kernel(lons, span, x_ref, wq_ref, wkv_ref, wo_ref, sel_ref, o_ref, x_s, o_s):
+def column_kernel(lons, span, unroll, x_ref, wq_ref, wkv_ref, wo_ref, sel_ref, o_ref, x_s, o_s):
     step = 2 * lons
     lats = sel_ref.shape[1]
     x_s[...] = x_ref[: lats * step].astype(F32)
@@ -114,15 +121,19 @@
                 o_s[hf, pl.ds(p * size + b * span, span), :] = part
         return 0
 
-    lax.fori_loop(0, lons, body, 0)
+    if unroll == lons:
+        for b in range(lons):
+            body(b, 0)
+    else:
+        lax.fori_loop(0, lons, body, 0, unroll=unroll)
     for p in range(o_ref.shape[0]):
         o_ref[p] = o_s[p % 2, p // 2 * size : (p // 2 + 1) * size].astype(BF)
 
 
-def column_attention(x, wq, wkv, wo, select, lons, span, peers):
+def column_attention(x, wq, wkv, wo, select, lons, span, peers, unroll=4):
     size = lons * span
     return pl.pallas_call(
-        functools.partial(column_kernel, lons, span),
+        functools.partial(column_kernel, lons, span, unroll),
         out_shape=jax.ShapeDtypeStruct((peers, size, 128), BF),
         in_specs=[VMEM] * 5,
         out_specs=VMEM,
@@ -136,20 +147,20 @@
 
 
 REACH = 15
+U_IN, U_OUT, U_LAST = 4, 4, 7
 S = 8
 HALO = 16
 
 
-def gelu(v):
-    half = 0.5 * v
-    return half + half * lax.erf(v * 0.7071067811865476)
+ROOT_HALF = 0.7071067811865476
 
 
 def taps_of(w_ref, level, half):
     out = []
     for k in range(9):
         both = w_ref[k, level : level + 1, :]
-        out.append(jnp.broadcast_to(jnp.where(half == 0, both[:, :128], both[:, 128:]), (S, 128)))
+        mine = jnp.where(half == 0, both[:, :128], both[:, 128:])
+        out.append(jnp.broadcast_to(mine * ROOT_HALF, (S, 128)))
     return out
 
 
@@ -157,12 +168,13 @@
     def cell(a, b):
         return src[pl.ds((i + (a - 1) * rate) * width + at + (b - 1) * rate, S), :]
 
-    total = None
+    lines = []
     for a in range(3):
-        for b in range(3):
-            term = taps[3 * a + b] * cell(a, b)
-            total = term if total is None else total + term
-    return (cell(1, 1) + gelu(total)).astype(BF).astype(F32)
+        terms = [taps[3 * a + b] * cell(a, b) for b in range(3)]
+        lines.append(terms[0] + terms[1] + terms[2])
+    total = lines[0] + lines[1] + lines[2]
+    part = ROOT_HALF * total
+    return (cell(1, 1) + part + part * lax.erf(total)).astype(BF)
 
 
 def spread(part, buf, width, lon, rows):
@@ -181,8 +193,18 @@
     return lax.shift_right_logical(index, 1) * (2 * rows) - REACH, lax.bitwise_and(index, 1)
 
 
-def valid(first, i, lats):
-    return jnp.logical_and(first + i >= 0, first + i < lats).astype(F32)
+def clear_outside(first, rows0, lats, clear):
+    def one(i, _):
+        clear(i)
+        return 0
+
+    @pl.when(first < 0)
+    def _():
+        lax.fori_loop(0, REACH, one, 0)
+
+    @pl.when(first + rows0 > lats)
+    def _():
+        lax.fori_loop(rows0 - REACH, rows0, one, 0)
 
 
 INNER = ((17, 25, 33, 41, 49, 57, 65, 71), (19, 27, 35, 43, 51, 59, 67, 69), (23, 31, 39, 47, 55, 63, 65))
@@ -202,7 +224,7 @@
         edge_ref[0, i] = jnp.concatenate(ends, 0).astype(BF)
         return 0
 
-    lax.fori_loop(0, rows0, raw, 0)
+    lax.fori_loop(0, rows0, raw, 0, unroll=2)
     src, dst = a_s, b_s
     edge = 0
     for level in range(3):
@@ -212,17 +234,23 @@
 
         def row(i, _, src=src, dst=dst, taps=taps, rate=rate, edge=edge, level=level):
             i = i + edge
-            mask = valid(first, i, lats)
-            out = [convolved(src, width, taps, i, c - HALO, rate) * mask for c in INNER[level]]
+            out = [convolved(src, width, taps, i, c - HALO, rate) for c in INNER[level]]
             if level < 2:
                 for c, v in zip(INNER[level], out):
-                    dst[pl.ds(i * width + c - HALO, S), :] = v
-                edge_ref[level + 1, i] = jnp.concatenate([out[0], out[-1]], 0).astype(BF)
+                    dst[pl.ds(i * width + c - HALO, S), :] = v.astype(F32)
+                edge_ref[level + 1, i] = jnp.concatenate([out[0], out[-1]], 0)
             else:
-                mid_ref[i - edge] = jnp.concatenate(out, 0).astype(BF)
+                mid_ref[i - edge] = jnp.concatenate(out, 0)
             return 0
 
-        lax.fori_loop(0, rows0 - 2 * edge, row, 0)
+        lax.fori_loop(0, rows0 - 2 * edge, row, 0, unroll=U_IN)
+
+        def clear(i, dst=dst, level=level):
+            if level < 2:
+                for c in range(0, width, S):
+                    dst[pl.ds(i * width + c, S), :] = jnp.zeros((S, 128), F32)
+
+        clear_outside(first, rows0, lats, clear)
         src, dst = dst, src
 
 
@@ -262,7 +290,7 @@
                 bufs[level][pl.ds(i * width + at[e], S), :] = both[e * S : e * S + S]
         return 0
 
-    lax.fori_loop(0, rows0, ends, 0)
+    lax.fori_loop(0, rows0, ends, 0, unroll=2)
 
     def middle(i, _):
         cells = mid_ref[i].astype(F32)
@@ -270,7 +298,7 @@
             bufs[3][pl.ds((i + 7) * width + c, S), :] = cells[g * S : g * S + S]
         return 0
 
-    lax.fori_loop(0, mid_ref.shape[0], middle, 0)
+    lax.fori_loop(0, mid_ref.shape[0], middle, 0, unroll=4)
     edge = 0
     for level in range(3):
         rate = 2**level
@@ -279,13 +307,18 @@
 
         def row(i, _, taps=taps, rate=rate, edge=edge, level=level):
             i = i + edge
-            mask = valid(first, i, lats)
-            out = [convolved(bufs[level], width, taps, i, c, rate) * mask for c in OUTER[level]]
+            out = [convolved(bufs[level], width, taps, i, c, rate) for c in OUTER[level]]
             for c, v in zip(OUTER[level], out):
-                bufs[level + 1][pl.ds(i * width + c, S), :] = v
+                bufs[level + 1][pl.ds(i * width + c, S), :] = v.astype(F32)
             return 0
 
-        lax.fori_loop(0, rows0 - 2 * edge, row, 0)
+        lax.fori_loop(0, rows0 - 2 * edge, row, 0, unroll=U_OUT)
+
+        def clear(i, level=level):
+            for c in range(0, width, S):
+                bufs[level + 1][pl.ds(i * width + c, S), :] = jnp.zeros((S, 128), F32)
+
+        clear_outside(first, rows0, lats, clear)
 
     taps = taps_of(w_ref, 3, half)
     for ref, base in ((send_ref, (1 - half) * rows), (keep_ref, half * rows)):
@@ -293,10 +326,10 @@
         def last(i, _, ref=ref, base=base):
             row = base + REACH + i
             out = [convolved(bufs[3], width, taps, row, HALO + q * S, 8) for q in range(cols // S)]
-            ref[i] = jnp.concatenate(out, 0).astype(BF)
+            ref[i] = jnp.concatenate(out, 0)
             return 0
 
-        lax.fori_loop(0, rows, last, 0)
+        lax.fori_loop(0, rows, last, 0, unroll=U_LAST)
 
 
 def outer_levels(left, right, edge, mid, taps, lats, rows, cols):
@@ -336,7 +369,7 @@
     lax.fori_loop(0, rows // batch, feed, 0)
 
 
-def feed_forward(keep, got, gate_up, down, batch=7):
+def feed_forward(keep, got, gate_up, down, batch=14):
     rows, cols, _ = keep.shape
     return pl.pallas_call(
         functools.partial(feed_kernel, batch),

time: 128 us -> 121 us (0.945)
  Pallas kernels: 38.5 us -> 31 us
    pallas_call x1, Pallas kernels: 7.49 us -> 4.74 us  [outer_levels(): pl.pallas_call(functools.partial(outer_kernel, lats), out_shape=(shape, s...]
    pallas_call x1, Pallas kernels: 8.37 us -> 6.54 us  [inner_levels(): pl.pallas_call(functools.partial(inner_kernel, lats, rows), out_shape=(ja...]
    pallas_call x1, Pallas kernels: 6.25 us -> 4.87 us  [column_attention(): pl.pallas_call(functools.partial(column_kernel, lons, span, unroll), out_...]
  transfers between devices with their start and end apart: 3 -> 3, of which waited for: 1 -> 1; matrix products, arithmetic and copies ran while one was open for 0% -> 0% of each run, Pallas kernels for 7% -> 5%
where the time goes in v3:
time: 121 us; the launch traced here: 120 us
  blocking collectives  77.1 us (64%)
  Pallas kernels  31 us (26%)
  starting transfers between devices  5.59 us (5%)
  waiting for transfers between devices  5.06 us (4%)
    all_to_all x1, blocking collectives, on_device(): lax.all_to_all(after_rows.reshape(n * m, 2 * lons, 128), ('lon', 'lat'),...  30.7 us
    all_to_all x1, blocking collectives, on_device(): own = lax.all_to_all(sent, 'lat', 0, 0, tiled=True)  28.7 us
    all_to_all x1, blocking collectives, on_device(): lax.all_to_all(padded, 'lon', 0, 0, tiled=True).reshape(n * cols, width)  17.7 us
    pallas_call x1, Pallas kernels, row_attention(): pl.pallas_call(functools.partial(row_kernel, qb), out_shape=jax.ShapeDtyp...  11.7 us
    pallas_call x1, Pallas kernels, inner_levels(): pl.pallas_call(functools.partial(inner_kernel, lats, rows), out_shape=(ja...  6.54 us
    ppermute x1, waiting for transfers between devices, on_device(): got = lax.ppermute(send, 'lat', [(i, i ^ 1) for i in range(m)])  5.05 us
    pallas_call x1, Pallas kernels, column_attention(): pl.pallas_call(functools.partial(column_kernel, lons, span, unroll), out_...  4.87 us
    pallas_call x1, Pallas kernels, outer_levels(): pl.pallas_call(functools.partial(outer_kernel, lats), out_shape=(shape, s...  4.74 us
  transfers between devices with their start and end apart: 3, of which 1 were waited for; matrix products, arithmetic and copies ran while one was open for 0% of the time, Pallas kernels for 5%

profile of v3, /device:TPU:7, one launch (start us, length us, event | category | flops | bytes accessed | tf_op | source)
XLA Modules:
  0.0 120.1 jit_solution(13987102352640813438)
XLA Ops:
  0.0 1.1 pad.4
  1.1 0.0 copy-start.4
  1.1 0.0 copy-start.5
  1.1 0.0 copy-start.6
  1.1 17.7 %all_to_all.15 = bf16[16,64,256]{2,1,0:T(8,128)(2,1)S(1)} all-to-all(bf16[16,64,256]{2,1,0:T(8,128)(2,1)S(1)} %pad.4), channel_id=1, replica_groups=mesh['lon'=16,'lat'=16] {'lon'}, dimensions={0} | all-to-all | bytes 1048576 | tf_op jit(solution)/shard_map/all_to_all | solution.py:414
  18.8 11.7 %row_attention.1 = bf16[2048,128]{1,0:T(8,128)(2,1)S(1)} custom-call(bf16[1024,256]{1,0:T(8,128)(2,1)S(1)} %bitcast.5, bf16[256,256]{1,0:T(8,128)(2,1)S(1)} %copy-done.5, bf16[256,512]{1,0:T(8,128)(2,1)S(1)} %copy-done.4, bf16[256,256]{1,0:T(8,128)(2,1)S(1)} %copy-done.6), custom_call_target="tpu_custom_call" | custom-call | tf_op jit(solution)/shard_map/row_attention/pallas_call | solution.py:85
  30.5 0.0 copy-start.2
  30.5 0.0 copy-start.3
  30.5 0.0 copy-start.7
  30.6 0.0 copy-start.8
  30.6 30.7 %all_to_all.16 = bf16[256,8,128]{2,1,0:T(8,128)(2,1)S(1)} all-to-all(bf16[256,8,128]{2,1,0:T(8,128)(2,1)S(1)} %bitcast.6), channel_id=1, replica_groups=mesh['lon'=16,'lat'=16] {'lon','lat'}, dimensions={0} | all-to-all | bytes 1048576 | tf_op jit(solution)/shard_map/all_to_all | solution.py:416
  61.3 4.9 %column_attention.1 = bf16[16,232,128]{2,1,0:T(8,128)(2,1)S(1)} custom-call(bf16[2048,128]{1,0:T(8,128)(2,1)S(1)} %bitcast.4, bf16[256,256]{1,0:T(8,128)(2,1)S(1)} %copy-done.7, bf16[256,512]{1,0:T(8,128)(2,1)S(1)} %copy-done.2, bf16[256,256]{1,0:T(8,128)(2,1)S(1)} %copy-done.8, bf16[512,224]{1,0:T(8,128)(2,1)S(1)} %copy-done.3), custom_call_target="tpu_custom_call" | custom-call | tf_op jit(solution)/shard_map/column_attention/pallas_call | solution.py:135
  66.2 28.7 %all_to_all.17.own_ref = bf16[16,232,128]{2,1,0:T(8,128)(2,1)S(1)} all-to-all(bf16[16,232,128]{2,1,0:T(8,128)(2,1)S(1)} %column_attention.1), channel_id=1, replica_groups=mesh['lon'=16,'lat'=16] {'lat'}, dimensions={0} | all-to-all | bytes 1900544 | tf_op jit(solution)/shard_map/all_to_all | solution.py:421
  94.9 2.1 %collective-permute-start.1 = (bf16[4,232,128]{2,1,0:T(8,128)(2,1)S(1)}, bf16[4,232,128]{2,1,0:T(8,128)(2,1)S(1)}, u32[]{:S(2)}, u32[]{:S(2)}) collective-permute-start(bf16[4,232,128]{2,1,0:T(8,128)(2,1)S(1)} %get-tuple-element.13), channel_id=1, source_target_pairs={{16,0},{32,16},{48,32},{64,48},{80,64},{96,80},{112,96},{128,112},... | collective-permute-start | bytes 712712 | tf_op jit(solution)/shard_map/ppermute | solution.py:424
  97.1 3.3 %collective-permute-start = (bf16[4,232,128]{2,1,0:T(8,128)(2,1)S(1)}, bf16[4,232,128]{2,1,0:T(8,128)(2,1)S(1)}, u32[]{:S(2)}, u32[]{:S(2)}) collective-permute-start(bf16[4,232,128]{2,1,0:T(8,128)(2,1)S(1)} %get-tuple-element.14), channel_id=1, source_target_pairs={{0,16},{16,32},{32,48},{48,64},{64,80},{80,96},{96,112},{112,128},... | collective-permute-start | bytes 712712 | tf_op jit(solution)/shard_map/ppermute | solution.py:423
  100.4 6.5 %inner_levels.1 = (bf16[3,58,16,128]{3,2,1,0:T(8,128)(2,1)S(1)}, bf16[44,56,128]{2,1,0:T(8,128)(2,1)S(1)}) custom-call(bf16[16,232,128]{2,1,0:T(8,128)(2,1)S(1)} %all_to_all.17.own_ref, f32[9,4,256]{2,1,0:T(4,128)S(1)} %bitcast.7), custom_call_target="tpu_custom_call" | custom-call | flops 60000000 | bytes 8000000 | tf_op jit(solution)/shard_map/inner_levels/pallas_call | solution.py:260
  106.9 0.0 copy-start
  106.9 0.0 collective-permute-done.1.right_ref
  106.9 0.0 collective-permute-done.left_ref
  107.0 0.0 copy-start.1
  107.0 4.7 %outer_levels.1 = (bf16[14,64,128]{2,1,0:T(8,128)(2,1)S(1)}, bf16[14,64,128]{2,1,0:T(8,128)(2,1)S(1)}) custom-call(bf16[4,232,128]{2,1,0:T(8,128)(2,1)S(1)} %collective-permute-done.left_ref, bf16[4,232,128]{2,1,0:T(8,128)(2,1)S(1)} %collective-permute-done.1.right_ref, bf16[3,58,16,128]{3,2,1,0:T(8,128)(2,1)S(1)} %get-tuple-element.9.edge_ref, ...), custom_call_target="tpu_custom_call" | custom-call | flops 40000000 | bytes 4000000 | tf_op jit(solution)/shard_map/outer_levels/pallas_call | solution.py:338
  111.7 0.2 collective-permute-start.2
  111.9 5.0 %collective-permute-done.2.got_ref = bf16[14,64,128]{2,1,0:T(8,128)(2,1)S(1)} collective-permute-done((bf16[14,64,128]{2,1,0:T(8,128)(2,1)S(1)}, bf16[14,64,128]{2,1,0:T(8,128)(2,1)S(1)}, u32[]{:S(2)}, u32[]{:S(2)}) %collective-permute-start.2) | collective-permute-done | bytes 229408 | tf_op jit(solution)/shard_map/ppermute | solution.py:428
  116.9 3.2 %feed_forward.1 = bf16[14,64,256]{2,1,0:T(8,128)(2,1)} custom-call(bf16[14,64,128]{2,1,0:T(8,128)(2,1)S(1)} %get-tuple-element.11.keep_ref, bf16[14,64,128]{2,1,0:T(8,128)(2,1)S(1)} %collective-permute-done.2.got_ref, bf16[256,2048]{1,0:T(8,128)(2,1)S(1)} %copy-done, bf16[1024,256]{1,0:T(8,128)(2,1)S(1)} %copy-done.1), custom_call_target="tpu_custom_call" | custom-call | tf_op jit(solution)/shard_map/feed_forward/pallas_call | solution.py:374
  (12 shorter events, 0.1 us)
Async XLA Ops:
  1.1 17.7 %copy-start.4 = (bf16[256,512]{1,0:T(8,128)(2,1)S(1)}, bf16[256,512]{1,0:T(8,128)(2,1)}, u32[]{:S(2)}) copy-start(bf16[256,512]{1,0:T(8,128)(2,1)} %wkv_ref.2) | copy-start | bytes 786436
  1.1 17.7 %copy-start.5 = (bf16[256,256]{1,0:T(8,128)(2,1)S(1)}, bf16[256,256]{1,0:T(8,128)(2,1)}, u32[]{:S(2)}) copy-start(bf16[256,256]{1,0:T(8,128)(2,1)} %wq_ref.2) | copy-start | bytes 393220
  1.1 17.7 %copy-start.6 = (bf16[256,256]{1,0:T(8,128)(2,1)S(1)}, bf16[256,256]{1,0:T(8,128)(2,1)}, u32[]{:S(2)}) copy-start(bf16[256,256]{1,0:T(8,128)(2,1)} %wo_ref.2) | copy-start | bytes 393220
  30.5 30.8 %copy-start.2 = (bf16[256,512]{1,0:T(8,128)(2,1)S(1)}, bf16[256,512]{1,0:T(8,128)(2,1)}, u32[]{:S(2)}) copy-start(bf16[256,512]{1,0:T(8,128)(2,1)} %wkv_ref.3) | copy-start | bytes 786436
  30.5 30.8 %copy-start.3 = (bf16[512,224]{1,0:T(8,128)(2,1)S(1)}, bf16[512,224]{1,0:T(8,128)(2,1)}, u32[]{:S(2)}) copy-start(bf16[512,224]{1,0:T(8,128)(2,1)} %constant.5.clone.sel_ref) | copy-start | bytes 688132
  30.5 30.7 %copy-start.7 = (bf16[256,256]{1,0:T(8,128)(2,1)S(1)}, bf16[256,256]{1,0:T(8,128)(2,1)}, u32[]{:S(2)}) copy-start(bf16[256,256]{1,0:T(8,128)(2,1)} %wq_ref.3) | copy-start | bytes 393220
  30.6 30.7 %copy-start.8 = (bf16[256,256]{1,0:T(8,128)(2,1)S(1)}, bf16[256,256]{1,0:T(8,128)(2,1)}, u32[]{:S(2)}) copy-start(bf16[256,256]{1,0:T(8,128)(2,1)} %wo_ref.3) | copy-start | bytes 393220
  94.9 5.5 %copy-start.9 = (f32[4,9,256]{2,0,1:T(4,128)S(1)}, f32[4,9,256]{2,0,1:T(4,128)}, u32[]{:S(2)}) copy-start(f32[4,9,256]{2,0,1:T(4,128)} %param.18) | copy-start | bytes 110596
  94.9 12.0 %collective-permute-start.1 = (bf16[4,232,128]{2,1,0:T(8,128)(2,1)S(1)}, bf16[4,232,128]{2,1,0:T(8,128)(2,1)S(1)}, u32[]{:S(2)}, u32[]{:S(2)}) collective-permute-start(bf16[4,232,128]{2,1,0:T(8,128)(2,1)S(1)} %get-tuple-element.13), channel_id=1, source_target_pairs={{16,0},{32,16},{48,32},{64,48},{80,64},{96,80},{112,96},{128,112},... | collective-permute-start | bytes 712712 | tf_op jit(solution)/shard_map/ppermute | solution.py:424
  97.1 9.9 %collective-permute-start = (bf16[4,232,128]{2,1,0:T(8,128)(2,1)S(1)}, bf16[4,232,128]{2,1,0:T(8,128)(2,1)S(1)}, u32[]{:S(2)}, u32[]{:S(2)}) collective-permute-start(bf16[4,232,128]{2,1,0:T(8,128)(2,1)S(1)} %get-tuple-element.14), channel_id=1, source_target_pairs={{0,16},{16,32},{32,48},{48,64},{64,80},{80,96},{96,112},{112,128},... | collective-permute-start | bytes 712712 | tf_op jit(solution)/shard_map/ppermute | solution.py:423
  106.9 10.0 %copy-start = (bf16[256,2048]{1,0:T(8,128)(2,1)S(1)}, bf16[256,2048]{1,0:T(8,128)(2,1)}, u32[]{:S(2)}) copy-start(bf16[256,2048]{1,0:T(8,128)(2,1)} %gu_ref.1) | copy-start | bytes 3145732
  107.0 10.0 %copy-start.1 = (bf16[1024,256]{1,0:T(8,128)(2,1)S(1)}, bf16[1024,256]{1,0:T(8,128)(2,1)}, u32[]{:S(2)}) copy-start(bf16[1024,256]{1,0:T(8,128)(2,1)} %down_ref.1) | copy-start | bytes 1572868
  111.7 5.2 %collective-permute-start.2 = (bf16[14,64,128]{2,1,0:T(8,128)(2,1)S(1)}, bf16[14,64,128]{2,1,0:T(8,128)(2,1)S(1)}, u32[]{:S(2)}, u32[]{:S(2)}) collective-permute-start(bf16[14,64,128]{2,1,0:T(8,128)(2,1)S(1)} %get-tuple-element.12), channel_id=1, source_target_pairs={{0,1},{1,0},{2,3},{3,2},{4,5},{5,4},{6,7},{7,6},{8,9},{9,8},{10,11... | collective-permute-start | bytes 688136 | tf_op jit(solution)/shard_map/ppermute | solution.py:428

commit v4 on v3

--- a/solution.py
+++ b/solution.py
@@ -27,16 +27,49 @@
     return jnp.dot(a, b, preferred_element_type=F32)
 
 
+def value_rows(values):
+    turned = jnp.transpose(values)
+    one = jnp.ones((16, values.shape[0]), BF)
+    return [jnp.concatenate([turned[32 * h : 32 * h + 32], one], 0) for h in range(HEADS)]
+
+
+def attend(q, keys, value_of, pieces=2):
+    lane = lax.broadcasted_iota(jnp.int32, (1, 256), 1) >> 5
+    size = q.shape[0] // pieces
+
+    def scores_of(h, z):
+        some = q[z * size : z * size + size]
+        masked = jnp.where(lane == h, some, jnp.zeros_like(some))
+        return lax.dot_general(keys, masked, NT, preferred_element_type=F32)
+
+    order = [(h, z) for h in range(HEADS) for z in range(pieces)]
+    parts = [[] for _ in range(pieces)]
+    later = scores_of(*order[0])
+    for at, (h, z) in enumerate(order):
+        scores = later
+        if at + 1 < len(order):
+            later = scores_of(*order[at + 1])
+        highest = jnp.max(scores, 0, keepdims=True)
+        weights = jnp.exp2((scores - highest) * SCALE).astype(BF)
+        sums = mm(value_of(h), weights)
+        parts[z].append(sums[:32] / sums[32:33])
+    whole = jnp.concatenate([jnp.concatenate(p, 0) for p in parts], 1)
+    return jnp.transpose(whole).astype(BF)
+
+
 def value_blocks(values):
     lane = lax.broadcasted_iota(jnp.int32, (1, 128), 1) >> 5
     one = jnp.ones((values.shape[0], 128), BF)
+    blocks = []
     for h in range(HEADS):
         group = values[:, 128 * (h // 4) : 128 * (h // 4) + 128]
-        yield h, jnp.concatenate([jnp.where(lane == h % 4, group, jnp.zeros_like(group)), one], -1)
-
-
-def attend(q, keys, value_of):
+        blocks.append(jnp.concatenate([jnp.where(lane == h % 4, group, jnp.zeros_like(group)), one], -1))
+    return blocks
+
+
+def attend_short(q, keys, values):
     lane = lax.broadcasted_iota(jnp.int32, (1, 256), 1) >> 5
+    blocks = value_blocks(values)
 
     def scores_of(h):
         masked = jnp.where(lane == h, q, jnp.zeros_like(q))
@@ -52,7 +85,7 @@
                 later = scores_of(h + 1)
             highest = jnp.max(scores, -1, keepdims=True)
             weights = jnp.exp2((scores - highest) * SCALE).astype(BF)
-            sums = mm(weights, value_of(h))
+            sums = mm(weights, blocks[h])
             part = sums[:, :128] / sums[:, 128:]
             total = part if total is None else total + part
         halves.append(total.astype(BF))
@@ -65,7 +98,7 @@
     q_s[...] = mm(n, wq_ref[...]).astype(BF)
     kv = mm(n, wkv_ref[...]).astype(BF)
     k_s[...] = kv[:, :256]
-    for h, block in value_blocks(kv[:, 256:]):
+    for h, block in enumerate(value_rows(kv[:, 256:])):
         v_s[h] = block
 
     def body(i, _):
@@ -80,7 +113,7 @@
     lax.fori_loop(0, rows // qb, body, 0)
 
 
-def row_attention(x, wq, wkv, wo, qb=512):
+def row_attention(x, wq, wkv, wo, qb=1024):
     rows = x.shape[0]
     return pl.pallas_call(
         functools.partial(row_kernel, qb),
@@ -90,7 +123,7 @@
         scratch_shapes=[
             pltpu.VMEM((rows, 256), BF),
             pltpu.VMEM((rows, 256), BF),
-            pltpu.VMEM((HEADS, rows, 256), BF),
+            pltpu.VMEM((HEADS, 48, rows), BF),
             pltpu.VMEM((2 * qb, 128), F32),
         ],
         compiler_params=pltpu.CompilerParams(vmem_limit_bytes=LIMIT),
@@ -111,8 +144,7 @@
         n = norm(x)
         q = mm(n, wq_ref[...]).astype(BF)
         kv = mm(n, wkv_ref[...]).astype(BF)
-        blocks_of = dict(value_blocks(kv[:, 256:]))
-        mixed = attend(q, kv[:, :256], lambda h: blocks_of[h])
+        mixed = attend_short(q, kv[:, :256], kv[:, 256:])
         after = (x + mm(mixed, wo_ref[...])).astype(BF)
         sent = mm(sel_ref[...], after)
         for p in range(blocks):
@@ -208,10 +240,11 @@
 
 
 INNER = ((17, 25, 33, 41, 49, 57, 65, 71), (19, 27, 35, 43, 51, 59, 67, 69), (23, 31, 39, 47, 55, 63, 65))
+MIDDLE = (2, 3, 4, 5)
 OUTER = ((2, 9, 79, 86), (4, 11, 77, 84), (8, 15, 73, 80))
 
 
-def inner_kernel(lats, rows, own_ref, w_ref, edge_ref, mid_ref, a_s, b_s):
+def inner_kernel(lats, rows, own_ref, w_ref, edge_ref, mid_ref, done_ref, a_s, b_s):
     first, half = position(rows)
     rows0 = edge_ref.shape[1]
     width = own_ref.shape[0] * own_ref.shape[1] // rows0
@@ -235,9 +268,9 @@
         def row(i, _, src=src, dst=dst, taps=taps, rate=rate, edge=edge, level=level):
             i = i + edge
             out = [convolved(src, width, taps, i, c - HALO, rate) for c in INNER[level]]
+            for c, v in zip(INNER[level], out):
+                dst[pl.ds(i * width + c - HALO, S), :] = v.astype(F32)
             if level < 2:
-                for c, v in zip(INNER[level], out):
-                    dst[pl.ds(i * width + c - HALO, S), :] = v.astype(F32)
                 edge_ref[level + 1, i] = jnp.concatenate([out[0], out[-1]], 0)
             else:
                 mid_ref[i - edge] = jnp.concatenate(out, 0)
@@ -245,13 +278,21 @@
 
         lax.fori_loop(0, rows0 - 2 * edge, row, 0, unroll=U_IN)
 
-        def clear(i, dst=dst, level=level):
-            if level < 2:
-                for c in range(0, width, S):
-                    dst[pl.ds(i * width + c, S), :] = jnp.zeros((S, 128), F32)
+        def clear(i, dst=dst):
+            for c in range(0, width, S):
+                dst[pl.ds(i * width + c, S), :] = jnp.zeros((S, 128), F32)
 
         clear_outside(first, rows0, lats, clear)
         src, dst = dst, src
+
+    taps = taps_of(w_ref, 3, half)
+
+    def last(i, _):
+        out = [convolved(src, width, taps, i + REACH, q * S, 8) for q in MIDDLE]
+        done_ref[i] = jnp.concatenate(out, 0)
+        return 0
+
+    lax.fori_loop(0, 2 * rows, last, 0, unroll=U_LAST)
 
 
 def inner_levels(own, taps, lats, rows):
@@ -262,9 +303,10 @@
         out_shape=(
             jax.ShapeDtypeStruct((3, rows0, 2 * S, 128), BF),
             jax.ShapeDtypeStruct((rows0 - 14, len(INNER[2]) * S, 128), BF),
+            jax.ShapeDtypeStruct((2 * rows, len(MIDDLE) * S, 128), BF),
         ),
         in_specs=[VMEM] * 2,
-        out_specs=(VMEM, VMEM),
+        out_specs=(VMEM, VMEM, VMEM),
         scratch_shapes=[pltpu.VMEM((per, 128), F32)] * 2,
         compiler_params=pltpu.CompilerParams(vmem_limit_bytes=LIMIT),
         cost_estimate=pl.CostEstimate(flops=60000000, bytes_accessed=8000000, transcendentals=1000000),
@@ -272,7 +314,7 @@
     )(own, taps)
 
 
-def outer_kernel(lats, left_ref, right_ref, edge_ref, mid_ref, w_ref, keep_ref, send_ref, *bufs):
+def outer_kernel(lats, left_ref, right_ref, edge_ref, mid_ref, done_ref, w_ref, keep_ref, send_ref, *bufs):
     rows, cols, _ = keep_ref.shape
     first, half = position(rows)
     rows0 = edge_ref.shape[1]
@@ -325,26 +367,30 @@
 
         def last(i, _, ref=ref, base=base):
             row = base + REACH + i
-            out = [convolved(bufs[3], width, taps, row, HALO + q * S, 8) for q in range(cols // S)]
+            out = [
+                done_ref[base + i] if q == MIDDLE[0] else convolved(bufs[3], width, taps, row, HALO + q * S, 8)
+                for q in range(cols // S)
+                if q not in MIDDLE[1:]
+            ]
             ref[i] = jnp.concatenate(out, 0)
             return 0
 
         lax.fori_loop(0, rows, last, 0, unroll=U_LAST)
 
 
-def outer_levels(left, right, edge, mid, taps, lats, rows, cols):
+def outer_levels(left, right, edge, mid, done, taps, lats, rows, cols):
     rows0 = edge.shape[1]
     shape = jax.ShapeDtypeStruct((rows, cols, 128), BF)
     return pl.pallas_call(
         functools.partial(outer_kernel, lats),
         out_shape=(shape, shape),
-        in_specs=[VMEM] * 5,
+        in_specs=[VMEM] * 6,
         out_specs=(VMEM, VMEM),
         scratch_shapes=[pltpu.VMEM((rows0 * (cols + 2 * HALO), 128), F32)] * 4,
         compiler_params=pltpu.CompilerParams(vmem_limit_bytes=LIMIT),
         cost_estimate=pl.CostEstimate(flops=40000000, bytes_accessed=4000000, transcendentals=500000),
         name="outer_levels",
-    )(left, right, edge, mid, taps)
+    )(left, right, edge, mid, done, taps)
 
 
 def feed_kernel(batch, keep_ref, got_ref, gu_ref, down_ref, o_ref):
@@ -423,8 +469,8 @@
     left = lax.ppermute(own[m - k :], "lon", [(i, (i + 1) % n) for i in range(n)])
     right = lax.ppermute(own[:k], "lon", [((i + 1) % n, i) for i in range(n)])
     taps = jnp.swapaxes(conv_kernel, 0, 1)
-    edge, mid = inner_levels(own, taps, rows * m, rows)
-    keep, send = outer_levels(left, right, edge, mid, taps, rows * m, rows, cols)
+    edge, mid, done = inner_levels(own, taps, rows * m, rows)
+    keep, send = outer_levels(left, right, edge, mid, done, taps, rows * m, rows, cols)
     got = lax.ppermute(send, "lat", [(i, i ^ 1) for i in range(m)])
     return feed_forward(keep, got, gate_up, down_proj)
 

time: 121 us -> 119 us (0.983)
  transfers between devices with their start and end apart: 3 -> 3, of which waited for: 1 -> 1; matrix products, arithmetic and copies ran while one was open for 0% -> 0% of each run, Pallas kernels for 5% -> 6%
where the time goes in v4:
time: 119 us
  blocking collectives  77.1 us (65%)
  Pallas kernels  30.1 us (25%)
  starting transfers between devices  5.59 us (5%)
  waiting for transfers between devices  5.06 us (4%)
    all_to_all x1, blocking collectives, on_device(): lax.all_to_all(after_rows.reshape(n * m, 2 * lons, 128), ('lon', 'lat'),...  30.7 us
    all_to_all x1, blocking collectives, on_device(): own = lax.all_to_all(sent, 'lat', 0, 0, tiled=True)  28.7 us
    all_to_all x1, blocking collectives, on_device(): lax.all_to_all(padded, 'lon', 0, 0, tiled=True).reshape(n * cols, width)  17.7 us
    pallas_call x1, Pallas kernels, row_attention(): pl.pallas_call(functools.partial(row_kernel, qb), out_shape=jax.ShapeDtyp...  10.5 us
    pallas_call x1, Pallas kernels, inner_levels(): pl.pallas_call(functools.partial(inner_kernel, lats, rows), out_shape=(ja...  7.12 us
    ppermute x1, waiting for transfers between devices, on_device(): got = lax.ppermute(send, 'lat', [(i, i ^ 1) for i in range(m)])  5.05 us
    pallas_call x1, Pallas kernels, column_attention(): pl.pallas_call(functools.partial(column_kernel, lons, span, unroll), out_...  4.87 us
    pallas_call x1, Pallas kernels, outer_levels(): pl.pallas_call(functools.partial(outer_kernel, lats), out_shape=(shape, s...  4.38 us
  transfers between devices with their start and end apart: 3, of which 1 were waited for; matrix products, arithmetic and copies ran while one was open for 0% of the time, Pallas kernels for 6%

profile of v4, /device:TPU:7, one launch (start us, length us, event | category | flops | bytes accessed | tf_op | source)
XLA Modules:
  0.0 119.1 jit_solution(1615610439974805582)
XLA Ops:
  0.0 1.1 pad.4
  1.1 0.0 copy-start.4
  1.1 0.0 copy-start.5
  1.1 0.0 copy-start.6
  1.1 17.7 %all_to_all.15 = bf16[16,64,256]{2,1,0:T(8,128)(2,1)S(1)} all-to-all(bf16[16,64,256]{2,1,0:T(8,128)(2,1)S(1)} %pad.4), channel_id=1, replica_groups=mesh['lon'=16,'lat'=16] {'lon'}, dimensions={0} | all-to-all | bytes 1048576 | tf_op jit(solution)/shard_map/all_to_all | solution.py:460
  18.8 10.5 %row_attention.1 = bf16[2048,128]{1,0:T(8,128)(2,1)S(1)} custom-call(bf16[1024,256]{1,0:T(8,128)(2,1)S(1)} %bitcast.5, bf16[256,256]{1,0:T(8,128)(2,1)S(1)} %copy-done.5, bf16[256,512]{1,0:T(8,128)(2,1)S(1)} %copy-done.4, bf16[256,256]{1,0:T(8,128)(2,1)S(1)} %copy-done.6), custom_call_target="tpu_custom_call" | custom-call | tf_op jit(solution)/shard_map/row_attention/pallas_call | solution.py:118
  29.3 0.0 copy-start.2
  29.3 0.0 copy-start.3
  29.4 0.0 copy-start.7
  29.4 0.0 copy-start.8
  29.4 30.7 %all_to_all.16 = bf16[256,8,128]{2,1,0:T(8,128)(2,1)S(1)} all-to-all(bf16[256,8,128]{2,1,0:T(8,128)(2,1)S(1)} %bitcast.6), channel_id=1, replica_groups=mesh['lon'=16,'lat'=16] {'lon','lat'}, dimensions={0} | all-to-all | bytes 1048576 | tf_op jit(solution)/shard_map/all_to_all | solution.py:462
  60.1 4.9 %column_attention.1 = bf16[16,232,128]{2,1,0:T(8,128)(2,1)S(1)} custom-call(bf16[2048,128]{1,0:T(8,128)(2,1)S(1)} %bitcast.4, bf16[256,256]{1,0:T(8,128)(2,1)S(1)} %copy-done.7, bf16[256,512]{1,0:T(8,128)(2,1)S(1)} %copy-done.2, bf16[256,256]{1,0:T(8,128)(2,1)S(1)} %copy-done.8, bf16[512,224]{1,0:T(8,128)(2,1)S(1)} %copy-done.3), custom_call_target="tpu_custom_call" | custom-call | tf_op jit(solution)/shard_map/column_attention/pallas_call | solution.py:167
  65.0 28.7 %all_to_all.17.own_ref = bf16[16,232,128]{2,1,0:T(8,128)(2,1)S(1)} all-to-all(bf16[16,232,128]{2,1,0:T(8,128)(2,1)S(1)} %column_attention.1), channel_id=1, replica_groups=mesh['lon'=16,'lat'=16] {'lat'}, dimensions={0} | all-to-all | bytes 1900544 | tf_op jit(solution)/shard_map/all_to_all | solution.py:467
  93.8 2.1 %collective-permute-start.1 = (bf16[4,232,128]{2,1,0:T(8,128)(2,1)S(1)}, bf16[4,232,128]{2,1,0:T(8,128)(2,1)S(1)}, u32[]{:S(2)}, u32[]{:S(2)}) collective-permute-start(bf16[4,232,128]{2,1,0:T(8,128)(2,1)S(1)} %get-tuple-element.15), channel_id=1, source_target_pairs={{16,0},{32,16},{48,32},{64,48},{80,64},{96,80},{112,96},{128,112},... | collective-permute-start | bytes 712712 | tf_op jit(solution)/shard_map/ppermute | solution.py:470
  95.9 3.3 %collective-permute-start = (bf16[4,232,128]{2,1,0:T(8,128)(2,1)S(1)}, bf16[4,232,128]{2,1,0:T(8,128)(2,1)S(1)}, u32[]{:S(2)}, u32[]{:S(2)}) collective-permute-start(bf16[4,232,128]{2,1,0:T(8,128)(2,1)S(1)} %get-tuple-element.16), channel_id=1, source_target_pairs={{0,16},{16,32},{32,48},{48,64},{64,80},{80,96},{96,112},{112,128},... | collective-permute-start | bytes 712712 | tf_op jit(solution)/shard_map/ppermute | solution.py:469
  99.2 7.1 %inner_levels.1 = (bf16[3,58,16,128]{3,2,1,0:T(8,128)(2,1)S(1)}, bf16[44,56,128]{2,1,0:T(8,128)(2,1)S(1)}, bf16[28,32,128]{2,1,0:T(8,128)(2,1)S(1)}) custom-call(bf16[16,232,128]{2,1,0:T(8,128)(2,1)S(1)} %all_to_all.17.own_ref, f32[9,4,256]{2,1,0:T(4,128)S(1)} %bitcast.7), custom_call_target="tpu_custom_call" | custom-call | flops 60000000 | bytes 8000000 | tf_op jit(solution)/shard_map/inner_levels/pallas_call | solution.py:301
  106.3 0.0 copy-start
  106.3 0.0 collective-permute-done.1.right_ref
  106.3 0.0 collective-permute-done.left_ref
  106.4 0.0 copy-start.1
  106.4 4.4 %outer_levels.1 = (bf16[14,64,128]{2,1,0:T(8,128)(2,1)S(1)}, bf16[14,64,128]{2,1,0:T(8,128)(2,1)S(1)}) custom-call(bf16[4,232,128]{2,1,0:T(8,128)(2,1)S(1)} %collective-permute-done.left_ref, bf16[4,232,128]{2,1,0:T(8,128)(2,1)S(1)} %collective-permute-done.1.right_ref, bf16[3,58,16,128]{3,2,1,0:T(8,128)(2,1)S(1)} %get-tuple-element.10.edge_ref, ...), custom_call_target="tpu_custom_call" | custom-call | flops 40000000 | bytes 4000000 | tf_op jit(solution)/shard_map/outer_levels/pallas_call | solution.py:384
  110.7 0.2 collective-permute-start.2
  110.9 5.0 %collective-permute-done.2.got_ref = bf16[14,64,128]{2,1,0:T(8,128)(2,1)S(1)} collective-permute-done((bf16[14,64,128]{2,1,0:T(8,128)(2,1)S(1)}, bf16[14,64,128]{2,1,0:T(8,128)(2,1)S(1)}, u32[]{:S(2)}, u32[]{:S(2)}) %collective-permute-start.2) | collective-permute-done | bytes 229408 | tf_op jit(solution)/shard_map/ppermute | solution.py:474
  116.0 3.2 %feed_forward.1 = bf16[14,64,256]{2,1,0:T(8,128)(2,1)} custom-call(bf16[14,64,128]{2,1,0:T(8,128)(2,1)S(1)} %get-tuple-element.13.keep_ref, bf16[14,64,128]{2,1,0:T(8,128)(2,1)S(1)} %collective-permute-done.2.got_ref, bf16[256,2048]{1,0:T(8,128)(2,1)S(1)} %copy-done, bf16[1024,256]{1,0:T(8,128)(2,1)S(1)} %copy-done.1), custom_call_target="tpu_custom_call" | custom-call | tf_op jit(solution)/shard_map/feed_forward/pallas_call | solution.py:420
  (12 shorter events, 0.1 us)
Async XLA Ops:
  1.1 17.7 %copy-start.4 = (bf16[256,512]{1,0:T(8,128)(2,1)S(1)}, bf16[256,512]{1,0:T(8,128)(2,1)}, u32[]{:S(2)}) copy-start(bf16[256,512]{1,0:T(8,128)(2,1)} %wkv_ref.2) | copy-start | bytes 786436
  1.1 17.7 %copy-start.5 = (bf16[256,256]{1,0:T(8,128)(2,1)S(1)}, bf16[256,256]{1,0:T(8,128)(2,1)}, u32[]{:S(2)}) copy-start(bf16[256,256]{1,0:T(8,128)(2,1)} %wq_ref.2) | copy-start | bytes 393220
  1.1 17.7 %copy-start.6 = (bf16[256,256]{1,0:T(8,128)(2,1)S(1)}, bf16[256,256]{1,0:T(8,128)(2,1)}, u32[]{:S(2)}) copy-start(bf16[256,256]{1,0:T(8,128)(2,1)} %wo_ref.2) | copy-start | bytes 393220
  29.3 30.8 %copy-start.2 = (bf16[256,512]{1,0:T(8,128)(2,1)S(1)}, bf16[256,512]{1,0:T(8,128)(2,1)}, u32[]{:S(2)}) copy-start(bf16[256,512]{1,0:T(8,128)(2,1)} %wkv_ref.3) | copy-start | bytes 786436
  29.3 30.8 %copy-start.3 = (bf16[512,224]{1,0:T(8,128)(2,1)S(1)}, bf16[512,224]{1,0:T(8,128)(2,1)}, u32[]{:S(2)}) copy-start(bf16[512,224]{1,0:T(8,128)(2,1)} %constant.5.clone.sel_ref) | copy-start | bytes 688132
  29.4 30.7 %copy-start.7 = (bf16[256,256]{1,0:T(8,128)(2,1)S(1)}, bf16[256,256]{1,0:T(8,128)(2,1)}, u32[]{:S(2)}) copy-start(bf16[256,256]{1,0:T(8,128)(2,1)} %wq_ref.3) | copy-start | bytes 393220
  29.4 30.7 %copy-start.8 = (bf16[256,256]{1,0:T(8,128)(2,1)S(1)}, bf16[256,256]{1,0:T(8,128)(2,1)}, u32[]{:S(2)}) copy-start(bf16[256,256]{1,0:T(8,128)(2,1)} %wo_ref.3) | copy-start | bytes 393220
  93.7 5.5 %copy-start.9 = (f32[4,9,256]{2,0,1:T(4,128)S(1)}, f32[4,9,256]{2,0,1:T(4,128)}, u32[]{:S(2)}) copy-start(f32[4,9,256]{2,0,1:T(4,128)} %param.18) | copy-start | bytes 110596
  93.8 12.6 %collective-permute-start.1 = (bf16[4,232,128]{2,1,0:T(8,128)(2,1)S(1)}, bf16[4,232,128]{2,1,0:T(8,128)(2,1)S(1)}, u32[]{:S(2)}, u32[]{:S(2)}) collective-permute-start(bf16[4,232,128]{2,1,0:T(8,128)(2,1)S(1)} %get-tuple-element.15), channel_id=1, source_target_pairs={{16,0},{32,16},{48,32},{64,48},{80,64},{96,80},{112,96},{128,112},... | collective-permute-start | bytes 712712 | tf_op jit(solution)/shard_map/ppermute | solution.py:470
  95.9 10.5 %collective-permute-start = (bf16[4,232,128]{2,1,0:T(8,128)(2,1)S(1)}, bf16[4,232,128]{2,1,0:T(8,128)(2,1)S(1)}, u32[]{:S(2)}, u32[]{:S(2)}) collective-permute-start(bf16[4,232,128]{2,1,0:T(8,128)(2,1)S(1)} %get-tuple-element.16), channel_id=1, source_target_pairs={{0,16},{16,32},{32,48},{48,64},{64,80},{80,96},{96,112},{112,128},... | collective-permute-start | bytes 712712 | tf_op jit(solution)/shard_map/ppermute | solution.py:469
  106.3 9.6 %copy-start = (bf16[256,2048]{1,0:T(8,128)(2,1)S(1)}, bf16[256,2048]{1,0:T(8,128)(2,1)}, u32[]{:S(2)}) copy-start(bf16[256,2048]{1,0:T(8,128)(2,1)} %gu_ref.1) | copy-start | bytes 3145732
  106.4 9.6 %copy-start.1 = (bf16[1024,256]{1,0:T(8,128)(2,1)S(1)}, bf16[1024,256]{1,0:T(8,128)(2,1)}, u32[]{:S(2)}) copy-start(bf16[1024,256]{1,0:T(8,128)(2,1)} %down_ref.1) | copy-start | bytes 1572868
  110.7 5.2 %collective-permute-start.2 = (bf16[14,64,128]{2,1,0:T(8,128)(2,1)S(1)}, bf16[14,64,128]{2,1,0:T(8,128)(2,1)S(1)}, u32[]{:S(2)}, u32[]{:S(2)}) collective-permute-start(bf16[14,64,128]{2,1,0:T(8,128)(2,1)S(1)} %get-tuple-element.14), channel_id=1, source_target_pairs={{0,1},{1,0},{2,3},{3,2},{4,5},{5,4},{6,7},{7,6},{8,9},{9,8},{10,11... | collective-permute-start | bytes 688136 | tf_op jit(solution)/shard_map/ppermute | solution.py:474

commit v5 on v4

--- a/solution.py
+++ b/solution.py
@@ -159,7 +159,7 @@
     else:
         lax.fori_loop(0, lons, body, 0, unroll=unroll)
     for p in range(o_ref.shape[0]):
-        o_ref[p] = o_s[p % 2, p // 2 * size : (p // 2 + 1) * size].astype(BF)
+        o_ref[p] = o_s[p // blocks, p % blocks * size : (p % blocks + 1) * size].astype(BF)
 
 
 def column_attention(x, wq, wkv, wo, select, lons, span, peers, unroll=4):
@@ -221,8 +221,7 @@
 
 
 def position(rows):
-    index = lax.axis_index("lat")
-    return lax.shift_right_logical(index, 1) * (2 * rows) - REACH, lax.bitwise_and(index, 1)
+    return lax.axis_index("block") * (2 * rows) - REACH, lax.axis_index("half")
 
 
 def clear_outside(first, rows0, lats, clear):
@@ -395,7 +394,7 @@
 
 def feed_kernel(batch, keep_ref, got_ref, gu_ref, down_ref, o_ref):
     rows, cols, _ = keep_ref.shape
-    half = lax.bitwise_and(lax.axis_index("lat"), 1)
+    half = lax.axis_index("half")
 
     def feed(c, _):
         sl = pl.ds(c * batch, batch)
@@ -436,7 +435,8 @@
         for r in range(span):
             lat = 2 * p * rows - REACH + r
             if 0 <= lat < lats:
-                pick[p * pitch + r, (lat % rows) * blocks + lat // rows] = 1
+                at = lat // rows
+                pick[p * pitch + r, (lat % rows) * blocks + at % 2 * (blocks // 2) + at // 2] = 1
     return pick.astype(BF)
 
 
@@ -454,32 +454,36 @@
 ):
     rows, cols, width = grid_state.shape
     n = lax.axis_size("lon")
-    m = lax.axis_size("lat")
+    m = 2 * lax.axis_size("block")
+    lat = ("half", "block")
     lons = cols // m
     padded = jnp.pad(grid_state, ((0, n - rows), (0, 0), (0, 0)))
     lines = lax.all_to_all(padded, "lon", 0, 0, tiled=True).reshape(n * cols, width)
     after_rows = row_attention(lines, row_query, row_keyval, row_output)
-    moved = lax.all_to_all(after_rows.reshape(n * m, 2 * lons, 128), ("lon", "lat"), 0, 0, tiled=True)
+    moved = lax.all_to_all(after_rows.reshape(n * m, 2 * lons, 128), ("lon",) + lat, 0, 0, tiled=True)
     moved = moved.reshape(-1, 128)
     pick = jnp.asarray(selection(rows * m, rows))
     span = 2 * rows + 2 * REACH
     sent = column_attention(moved, column_query, column_keyval, column_output, pick, lons, span, m)
-    own = lax.all_to_all(sent, "lat", 0, 0, tiled=True)
+    own = lax.all_to_all(sent, lat, 0, 0, tiled=True)
     k = HALO // lons
     left = lax.ppermute(own[m - k :], "lon", [(i, (i + 1) % n) for i in range(n)])
     right = lax.ppermute(own[:k], "lon", [((i + 1) % n, i) for i in range(n)])
     taps = jnp.swapaxes(conv_kernel, 0, 1)
     edge, mid, done = inner_levels(own, taps, rows * m, rows)
     keep, send = outer_levels(left, right, edge, mid, done, taps, rows * m, rows, cols)
-    got = lax.ppermute(send, "lat", [(i, i ^ 1) for i in range(m)])
+    got = lax.ppermute(send, "half", [(0, 1), (1, 0)])
     return feed_forward(keep, got, gate_up, down_proj)
 
 
 def solution(mesh):
+    n, m = mesh.devices.shape
+    pairs = jax.sharding.Mesh(mesh.devices.reshape(n, m // 2, 2), ("lon", "block", "half"))
+    cells = P(("block", "half"), "lon", None)
     return jax.shard_map(
         on_device,
-        mesh=mesh,
-        in_specs=(P("lat", "lon", None), P(), P(), P(), P(), P(), P(), P(), P(), P()),
-        out_specs=P("lat", "lon", None),
+        mesh=pairs,
+        in_specs=(cells, P(), P(), P(), P(), P(), P(), P(), P(), P()),
+        out_specs=cells,
         check_vma=False,
     )

time: 119 us -> 119 us (level); the launches traced: 119 us -> 117 us
  blocking collectives: 77.1 us -> 74 us
    all_to_all x2, blocking collectives: 59.4 us -> 56.4 us  [the longest x1 30.5 us: on_device(): lax.all_to_all(after_rows.reshape(n * m, 2 * lons, 128), ('lon',) + lat,...]
where the time goes in v5:
time: 119 us; the launch traced here: 117 us
  blocking collectives  74 us (62%)
  Pallas kernels  30.1 us (25%)
  starting transfers between devices  6.26 us (5%)
  waiting for transfers between devices  5.08 us (4%)
    all_to_all x1, blocking collectives, on_device(): lax.all_to_all(after_rows.reshape(n * m, 2 * lons, 128), ('lon',) + lat,...  30.5 us
    all_to_all x1, blocking collectives, on_device(): own = lax.all_to_all(sent, lat, 0, 0, tiled=True)  25.9 us
    all_to_all x1, blocking collectives, on_device(): lax.all_to_all(padded, 'lon', 0, 0, tiled=True).reshape(n * cols, width)  17.7 us
    pallas_call x1, Pallas kernels, row_attention(): pl.pallas_call(functools.partial(row_kernel, qb), out_shape=jax.ShapeDtyp...  10.5 us
    pallas_call x1, Pallas kernels, inner_levels(): pl.pallas_call(functools.partial(inner_kernel, lats, rows), out_shape=(ja...  7.12 us
    ppermute x1, waiting for transfers between devices, on_device(): got = lax.ppermute(send, 'half', [(0, 1), (1, 0)])  5.08 us
    pallas_call x1, Pallas kernels, column_attention(): pl.pallas_call(functools.partial(column_kernel, lons, span, unroll), out_...  4.86 us
    pallas_call x1, Pallas kernels, outer_levels(): pl.pallas_call(functools.partial(outer_kernel, lats), out_shape=(shape, s...  4.38 us
  transfers between devices with their start and end apart: 3, of which 1 were waited for; matrix products, arithmetic and copies ran while one was open for 0% of the time, Pallas kernels for 6%

profile of v5, /device:TPU:7, one launch (start us, length us, event | category | flops | bytes accessed | tf_op | source)
XLA Modules:
  0.0 116.7 jit_solution(9783120302321296877)
XLA Ops:
  0.0 1.1 pad.4
  1.1 0.0 copy-start.4
  1.1 0.0 copy-start.5
  1.1 0.0 copy-start.6
  1.1 17.7 %all_to_all.15 = bf16[16,64,256]{2,1,0:T(8,128)(2,1)S(1)} all-to-all(bf16[16,64,256]{2,1,0:T(8,128)(2,1)S(1)} %pad.4), channel_id=1, replica_groups=mesh['lon'=16,'block'=8,'half'=2] {'lon'}, dimensions={0} | all-to-all | bytes 1048576 | tf_op jit(solution)/shard_map/all_to_all | solution.py:461
  18.8 10.5 %row_attention.1 = bf16[2048,128]{1,0:T(8,128)(2,1)S(1)} custom-call(bf16[1024,256]{1,0:T(8,128)(2,1)S(1)} %bitcast.5, bf16[256,256]{1,0:T(8,128)(2,1)S(1)} %copy-done.5, bf16[256,512]{1,0:T(8,128)(2,1)S(1)} %copy-done.4, bf16[256,256]{1,0:T(8,128)(2,1)S(1)} %copy-done.6), custom_call_target="tpu_custom_call" | custom-call | tf_op jit(solution)/shard_map/row_attention/pallas_call | solution.py:118
  29.3 0.0 copy-start.2
  29.3 0.0 copy-start.3
  29.4 0.0 copy-start.7
  29.4 0.0 copy-start.8
  29.4 30.5 %all_to_all.16 = bf16[256,8,128]{2,1,0:T(8,128)(2,1)S(1)} all-to-all(bf16[256,8,128]{2,1,0:T(8,128)(2,1)S(1)} %bitcast.6), channel_id=1, replica_groups=mesh['lon'=16,'block'=8,'half'=2] {'lon','half','block'}, dimensions={0} | all-to-all | bytes 1048576 | tf_op jit(solution)/shard_map/all_to_all | solution.py:463
  59.9 4.9 %column_attention.1 = bf16[16,232,128]{2,1,0:T(8,128)(2,1)S(1)} custom-call(bf16[2048,128]{1,0:T(8,128)(2,1)S(1)} %bitcast.4, bf16[256,256]{1,0:T(8,128)(2,1)S(1)} %copy-done.7, bf16[256,512]{1,0:T(8,128)(2,1)S(1)} %copy-done.2, bf16[256,256]{1,0:T(8,128)(2,1)S(1)} %copy-done.8, bf16[512,224]{1,0:T(8,128)(2,1)S(1)} %copy-done.3), custom_call_target="tpu_custom_call" | custom-call | tf_op jit(solution)/shard_map/column_attention/pallas_call | solution.py:167
  64.7 25.9 %all_to_all.17.own_ref = bf16[16,232,128]{2,1,0:T(8,128)(2,1)S(1)} all-to-all(bf16[16,232,128]{2,1,0:T(8,128)(2,1)S(1)} %column_attention.1), channel_id=1, replica_groups=mesh['lon'=16,'block'=8,'half'=2] {'half','block'}, dimensions={0} | all-to-all | bytes 1900544 | tf_op jit(solution)/shard_map/all_to_all | solution.py:468
  90.7 2.8 %collective-permute-start.1 = (bf16[4,232,128]{2,1,0:T(8,128)(2,1)S(1)}, bf16[4,232,128]{2,1,0:T(8,128)(2,1)S(1)}, u32[]{:S(2)}, u32[]{:S(2)}) collective-permute-start(bf16[4,232,128]{2,1,0:T(8,128)(2,1)S(1)} %get-tuple-element.15), channel_id=1, source_target_pairs={{16,0},{32,16},{48,32},{64,48},{80,64},{96,80},{112,96},{128,112},... | collective-permute-start | bytes 712712 | tf_op jit(solution)/shard_map/ppermute | solution.py:471
  93.5 3.2 %collective-permute-start = (bf16[4,232,128]{2,1,0:T(8,128)(2,1)S(1)}, bf16[4,232,128]{2,1,0:T(8,128)(2,1)S(1)}, u32[]{:S(2)}, u32[]{:S(2)}) collective-permute-start(bf16[4,232,128]{2,1,0:T(8,128)(2,1)S(1)} %get-tuple-element.16), channel_id=1, source_target_pairs={{0,16},{16,32},{32,48},{48,64},{64,80},{80,96},{96,112},{112,128},... | collective-permute-start | bytes 712712 | tf_op jit(solution)/shard_map/ppermute | solution.py:470
  96.6 7.1 %inner_levels.1 = (bf16[3,58,16,128]{3,2,1,0:T(8,128)(2,1)S(1)}, bf16[44,56,128]{2,1,0:T(8,128)(2,1)S(1)}, bf16[28,32,128]{2,1,0:T(8,128)(2,1)S(1)}) custom-call(bf16[16,232,128]{2,1,0:T(8,128)(2,1)S(1)} %all_to_all.17.own_ref, f32[9,4,256]{2,1,0:T(4,128)S(1)} %bitcast.7), custom_call_target="tpu_custom_call" | custom-call | flops 60000000 | bytes 8000000 | tf_op jit(solution)/shard_map/inner_levels/pallas_call | solution.py:300
  103.8 0.0 copy-start
  103.8 0.0 collective-permute-done.1.right_ref
  103.8 0.0 collective-permute-done.left_ref
  103.8 0.0 copy-start.1
  103.8 4.4 %outer_levels.1 = (bf16[14,64,128]{2,1,0:T(8,128)(2,1)S(1)}, bf16[14,64,128]{2,1,0:T(8,128)(2,1)S(1)}) custom-call(bf16[4,232,128]{2,1,0:T(8,128)(2,1)S(1)} %collective-permute-done.left_ref, bf16[4,232,128]{2,1,0:T(8,128)(2,1)S(1)} %collective-permute-done.1.right_ref, bf16[3,58,16,128]{3,2,1,0:T(8,128)(2,1)S(1)} %get-tuple-element.10.edge_ref, ...), custom_call_target="tpu_custom_call" | custom-call | flops 40000000 | bytes 4000000 | tf_op jit(solution)/shard_map/outer_levels/pallas_call | solution.py:383
  108.2 0.3 collective-permute-start.2
  108.5 5.1 %collective-permute-done.2.got_ref = bf16[14,64,128]{2,1,0:T(8,128)(2,1)S(1)} collective-permute-done((bf16[14,64,128]{2,1,0:T(8,128)(2,1)S(1)}, bf16[14,64,128]{2,1,0:T(8,128)(2,1)S(1)}, u32[]{:S(2)}, u32[]{:S(2)}) %collective-permute-start.2) | collective-permute-done | bytes 229408 | tf_op jit(solution)/shard_map/ppermute | solution.py:475
  113.6 3.2 %feed_forward.1 = bf16[14,64,256]{2,1,0:T(8,128)(2,1)} custom-call(bf16[14,64,128]{2,1,0:T(8,128)(2,1)S(1)} %get-tuple-element.13.keep_ref, bf16[14,64,128]{2,1,0:T(8,128)(2,1)S(1)} %collective-permute-done.2.got_ref, bf16[256,2048]{1,0:T(8,128)(2,1)S(1)} %copy-done, bf16[1024,256]{1,0:T(8,128)(2,1)S(1)} %copy-done.1), custom_call_target="tpu_custom_call" | custom-call | tf_op jit(solution)/shard_map/feed_forward/pallas_call | solution.py:419
  (12 shorter events, 0.1 us)
Async XLA Ops:
  1.1 17.7 %copy-start.4 = (bf16[256,512]{1,0:T(8,128)(2,1)S(1)}, bf16[256,512]{1,0:T(8,128)(2,1)}, u32[]{:S(2)}) copy-start(bf16[256,512]{1,0:T(8,128)(2,1)} %wkv_ref.2) | copy-start | bytes 786436
  1.1 17.7 %copy-start.5 = (bf16[256,256]{1,0:T(8,128)(2,1)S(1)}, bf16[256,256]{1,0:T(8,128)(2,1)}, u32[]{:S(2)}) copy-start(bf16[256,256]{1,0:T(8,128)(2,1)} %wq_ref.2) | copy-start | bytes 393220
  1.1 17.7 %copy-start.6 = (bf16[256,256]{1,0:T(8,128)(2,1)S(1)}, bf16[256,256]{1,0:T(8,128)(2,1)}, u32[]{:S(2)}) copy-start(bf16[256,256]{1,0:T(8,128)(2,1)} %wo_ref.2) | copy-start | bytes 393220
  29.3 30.5 %copy-start.2 = (bf16[256,512]{1,0:T(8,128)(2,1)S(1)}, bf16[256,512]{1,0:T(8,128)(2,1)}, u32[]{:S(2)}) copy-start(bf16[256,512]{1,0:T(8,128)(2,1)} %wkv_ref.3) | copy-start | bytes 786436
  29.3 30.5 %copy-start.3 = (bf16[512,224]{1,0:T(8,128)(2,1)S(1)}, bf16[512,224]{1,0:T(8,128)(2,1)}, u32[]{:S(2)}) copy-start(bf16[512,224]{1,0:T(8,128)(2,1)} %constant.5.clone.sel_ref) | copy-start | bytes 688132
  29.4 30.5 %copy-start.7 = (bf16[256,256]{1,0:T(8,128)(2,1)S(1)}, bf16[256,256]{1,0:T(8,128)(2,1)}, u32[]{:S(2)}) copy-start(bf16[256,256]{1,0:T(8,128)(2,1)} %wq_ref.3) | copy-start | bytes 393220
  29.4 30.5 %copy-start.8 = (bf16[256,256]{1,0:T(8,128)(2,1)S(1)}, bf16[256,256]{1,0:T(8,128)(2,1)}, u32[]{:S(2)}) copy-start(bf16[256,256]{1,0:T(8,128)(2,1)} %wo_ref.3) | copy-start | bytes 393220
  90.6 6.0 %copy-start.9 = (f32[4,9,256]{2,0,1:T(4,128)S(1)}, f32[4,9,256]{2,0,1:T(4,128)}, u32[]{:S(2)}) copy-start(f32[4,9,256]{2,0,1:T(4,128)} %param.18) | copy-start | bytes 110596
  90.7 13.1 %collective-permute-start.1 = (bf16[4,232,128]{2,1,0:T(8,128)(2,1)S(1)}, bf16[4,232,128]{2,1,0:T(8,128)(2,1)S(1)}, u32[]{:S(2)}, u32[]{:S(2)}) collective-permute-start(bf16[4,232,128]{2,1,0:T(8,128)(2,1)S(1)} %get-tuple-element.15), channel_id=1, source_target_pairs={{16,0},{32,16},{48,32},{64,48},{80,64},{96,80},{112,96},{128,112},... | collective-permute-start | bytes 712712 | tf_op jit(solution)/shard_map/ppermute | solution.py:471
  93.5 10.3 %collective-permute-start = (bf16[4,232,128]{2,1,0:T(8,128)(2,1)S(1)}, bf16[4,232,128]{2,1,0:T(8,128)(2,1)S(1)}, u32[]{:S(2)}, u32[]{:S(2)}) collective-permute-start(bf16[4,232,128]{2,1,0:T(8,128)(2,1)S(1)} %get-tuple-element.16), channel_id=1, source_target_pairs={{0,16},{16,32},{32,48},{48,64},{64,80},{80,96},{96,112},{112,128},... | collective-permute-start | bytes 712712 | tf_op jit(solution)/shard_map/ppermute | solution.py:470
  103.8 9.8 %copy-start = (bf16[256,2048]{1,0:T(8,128)(2,1)S(1)}, bf16[256,2048]{1,0:T(8,128)(2,1)}, u32[]{:S(2)}) copy-start(bf16[256,2048]{1,0:T(8,128)(2,1)} %gu_ref.1) | copy-start | bytes 3145732
  103.8 9.8 %copy-start.1 = (bf16[1024,256]{1,0:T(8,128)(2,1)S(1)}, bf16[1024,256]{1,0:T(8,128)(2,1)}, u32[]{:S(2)}) copy-start(bf16[1024,256]{1,0:T(8,128)(2,1)} %down_ref.1) | copy-start | bytes 1572868
  108.2 5.4 %collective-permute-start.2 = (bf16[14,64,128]{2,1,0:T(8,128)(2,1)S(1)}, bf16[14,64,128]{2,1,0:T(8,128)(2,1)S(1)}, u32[]{:S(2)}, u32[]{:S(2)}) collective-permute-start(bf16[14,64,128]{2,1,0:T(8,128)(2,1)S(1)} %get-tuple-element.14), channel_id=1, source_target_pairs={{0,1},{1,0},{2,3},{3,2},{4,5},{5,4},{6,7},{7,6},{8,9},{9,8},{10,11... | collective-permute-start | bytes 688136 | tf_op jit(solution)/shard_map/ppermute | solution.py:475

commit v6 on v5

--- a/solution.py
+++ b/solution.py
@@ -313,7 +313,7 @@
     )(own, taps)
 
 
-def outer_kernel(lats, left_ref, right_ref, edge_ref, mid_ref, done_ref, w_ref, keep_ref, send_ref, *bufs):
+def outer_kernel(lats, left_ref, right_ref, edge_ref, mid_ref, done_ref, w_ref, keep_ref, near_ref, far_ref, *bufs):
     rows, cols, _ = keep_ref.shape
     first, half = position(rows)
     rows0 = edge_ref.shape[1]
@@ -362,7 +362,8 @@
         clear_outside(first, rows0, lats, clear)
 
     taps = taps_of(w_ref, 3, half)
-    for ref, base in ((send_ref, (1 - half) * rows), (keep_ref, half * rows)):
+    other = (1 - half) * rows
+    for ref, base in ((near_ref, other), (far_ref, other + rows // 2), (keep_ref, half * rows)):
 
         def last(i, _, ref=ref, base=base):
             row = base + REACH + i
@@ -374,17 +375,17 @@
             ref[i] = jnp.concatenate(out, 0)
             return 0
 
-        lax.fori_loop(0, rows, last, 0, unroll=U_LAST)
+        lax.fori_loop(0, ref.shape[0], last, 0, unroll=U_LAST)
 
 
 def outer_levels(left, right, edge, mid, done, taps, lats, rows, cols):
     rows0 = edge.shape[1]
-    shape = jax.ShapeDtypeStruct((rows, cols, 128), BF)
+    shapes = [jax.ShapeDtypeStruct((r, cols, 128), BF) for r in (rows, rows // 2, rows // 2)]
     return pl.pallas_call(
         functools.partial(outer_kernel, lats),
-        out_shape=(shape, shape),
+        out_shape=shapes,
         in_specs=[VMEM] * 6,
-        out_specs=(VMEM, VMEM),
+        out_specs=[VMEM] * 3,
         scratch_shapes=[pltpu.VMEM((rows0 * (cols + 2 * HALO), 128), F32)] * 4,
         compiler_params=pltpu.CompilerParams(vmem_limit_bytes=LIMIT),
         cost_estimate=pl.CostEstimate(flops=40000000, bytes_accessed=4000000, transcendentals=500000),
@@ -392,38 +393,38 @@
     )(left, right, edge, mid, done, taps)
 
 
-def feed_kernel(batch, keep_ref, got_ref, gu_ref, down_ref, o_ref):
-    rows, cols, _ = keep_ref.shape
+def feed_kernel(part, keep_ref, got_ref, gu_ref, down_ref, *refs):
+    o_ref, o_s, sem = refs[-3:]
+    rows, cols, _ = got_ref.shape
     half = lax.axis_index("half")
-
-    def feed(c, _):
-        sl = pl.ds(c * batch, batch)
-        keep = keep_ref[sl].reshape(batch * cols, 128)
-        got = got_ref[sl].reshape(batch * cols, 128)
-        state = jnp.concatenate(
-            [jnp.where(half == 0, keep, got), jnp.where(half == 0, got, keep)], -1
-        ).astype(F32)
-        both = mm(norm(state), gu_ref[...])
-        units = gu_ref.shape[1] // 2
-        gate, up = both[:, :units], both[:, units:]
-        hidden = (gate / (1.0 + jnp.exp(-gate)) * up).astype(BF)
-        out = (state + mm(hidden, down_ref[...])).astype(BF)
-        o_ref[sl] = out.reshape(batch, cols, 256)
-        return 0
-
-    lax.fori_loop(0, rows // batch, feed, 0)
-
-
-def feed_forward(keep, got, gate_up, down, batch=14):
-    rows, cols, _ = keep.shape
+    keep = keep_ref[part * rows : part * rows + rows].reshape(rows * cols, 128)
+    got = got_ref[...].reshape(rows * cols, 128)
+    state = jnp.concatenate([jnp.where(half == 0, keep, got), jnp.where(half == 0, got, keep)], -1).astype(F32)
+    both = mm(norm(state), gu_ref[...])
+    units = gu_ref.shape[1] // 2
+    gate, up = both[:, :units], both[:, units:]
+    hidden = (gate / (1.0 + jnp.exp(-gate)) * up).astype(BF)
+    out = (state + mm(hidden, down_ref[...])).astype(BF)
+    o_s[...] = out.reshape(rows, cols, 256)
+    copy = pltpu.make_async_copy(o_s, o_ref.at[pl.ds(part * rows, rows)], sem)
+    copy.start()
+    copy.wait()
+
+
+def feed_forward(part, keep, got, gate_up, down, before=None):
+    anywhere = pl.BlockSpec(memory_space=pl.ANY)
+    more = [] if before is None else [before]
     return pl.pallas_call(
-        functools.partial(feed_kernel, batch),
-        out_shape=jax.ShapeDtypeStruct((rows, cols, 256), BF),
-        in_specs=[VMEM] * 4,
-        out_specs=VMEM,
+        functools.partial(feed_kernel, part),
+        out_shape=jax.ShapeDtypeStruct(keep.shape[:2] + (256,), BF),
+        in_specs=[VMEM] * 4 + [anywhere] * len(more),
+        out_specs=anywhere,
+        scratch_shapes=[pltpu.VMEM(got.shape[:2] + (256,), BF), pltpu.SemaphoreType.DMA],
+        input_output_aliases={4: 0} if more else {},
         compiler_params=pltpu.CompilerParams(vmem_limit_bytes=LIMIT),
+        cost_estimate=pl.CostEstimate(flops=700000000, bytes_accessed=2000000, transcendentals=500000),
         name="feed_forward",
-    )(keep, got, gate_up, down)
+    )(keep, got, gate_up, down, *more)
 
 
 def selection(lats, rows):
@@ -471,9 +472,11 @@
     right = lax.ppermute(own[:k], "lon", [((i + 1) % n, i) for i in range(n)])
     taps = jnp.swapaxes(conv_kernel, 0, 1)
     edge, mid, done = inner_levels(own, taps, rows * m, rows)
-    keep, send = outer_levels(left, right, edge, mid, done, taps, rows * m, rows, cols)
-    got = lax.ppermute(send, "half", [(0, 1), (1, 0)])
-    return feed_forward(keep, got, gate_up, down_proj)
+    keep, near, far = outer_levels(left, right, edge, mid, done, taps, rows * m, rows, cols)
+    swap = [(0, 1), (1, 0)]
+    got = [lax.ppermute(part, "half", swap) for part in (near, far)]
+    out = feed_forward(0, keep, got[0], gate_up, down_proj)
+    return feed_forward(1, keep, got[1], gate_up, down_proj, out)
 
 
 def solution(mesh):

time: 119 us -> 118 us (level)
  waiting for transfers between devices: 5.08 us -> 2.59 us
  starting transfers between devices: 6.26 us -> 7.52 us
    ppermute x1 -> x2, waiting for transfers between devices: 5.08 us -> 2.59 us  [on_device(): got = [lax.ppermute(part, 'half', swap) for part in (near, far)]]
    ppermute x1 -> x2, starting transfers between devices: 0.29 us -> 1.55 us  [on_device(): got = [lax.ppermute(part, 'half', swap) for part in (near, far)]]
    pallas_call x2 -> x3, Pallas kernels: 7.54 us -> 8.53 us  [the longest x1 4.36 us: outer_levels(): pl.pallas_call(functools.partial(outer_kernel, lats), out_shape=shapes, i...]
  transfers between devices with their start and end apart: 3 -> 4, of which waited for: 1 -> 1; matrix products, arithmetic and copies ran while one was open for 0% -> 0% of each run, Pallas kernels for 6% -> 8%
where the time goes in v6:
time: 118 us; the launch traced here: 117 us
  blocking collectives  74 us (63%)
  Pallas kernels  31.1 us (26%)
  starting transfers between devices  7.52 us (6%)
  waiting for transfers between devices  2.59 us (2%)
    all_to_all x1, blocking collectives, on_device(): lax.all_to_all(after_rows.reshape(n * m, 2 * lons, 128), ('lon',) + lat,...  30.5 us
    all_to_all x1, blocking collectives, on_device(): own = lax.all_to_all(sent, lat, 0, 0, tiled=True)  25.9 us
    all_to_all x1, blocking collectives, on_device(): lax.all_to_all(padded, 'lon', 0, 0, tiled=True).reshape(n * cols, width)  17.7 us
    pallas_call x1, Pallas kernels, row_attention(): pl.pallas_call(functools.partial(row_kernel, qb), out_shape=jax.ShapeDtyp...  10.5 us
    pallas_call x1, Pallas kernels, inner_levels(): pl.pallas_call(functools.partial(inner_kernel, lats, rows), out_shape=(ja...  7.12 us
    pallas_call x1, Pallas kernels, column_attention(): pl.pallas_call(functools.partial(column_kernel, lons, span, unroll), out_...  4.86 us
    pallas_call x1, Pallas kernels, outer_levels(): pl.pallas_call(functools.partial(outer_kernel, lats), out_shape=shapes, i...  4.36 us
    pallas_call x2, Pallas kernels, feed_forward(): pl.pallas_call(functools.partial(feed_kernel, part), out_shape=jax.ShapeD...  4.17 us
  transfers between devices with their start and end apart: 4, of which 1 were waited for; matrix products, arithmetic and copies ran while one was open for 0% of the time, Pallas kernels for 8%

profile of v6, /device:TPU:7, one launch (start us, length us, event | category | flops | bytes accessed | tf_op | source)
XLA Modules:
  0.0 116.7 jit_solution(11139819837414975643)
XLA Ops:
  0.0 1.1 pad.4
  1.1 0.0 copy-start.4
  1.1 0.0 copy-start.5
  1.1 0.0 copy-start.6
  1.1 17.7 %all_to_all.15 = bf16[16,64,256]{2,1,0:T(8,128)(2,1)S(1)} all-to-all(bf16[16,64,256]{2,1,0:T(8,128)(2,1)S(1)} %pad.4), channel_id=1, replica_groups=mesh['lon'=16,'block'=8,'half'=2] {'lon'}, dimensions={0} | all-to-all | bytes 1048576 | tf_op jit(solution)/shard_map/all_to_all | solution.py:462
  18.8 10.5 %row_attention.1 = bf16[2048,128]{1,0:T(8,128)(2,1)S(1)} custom-call(bf16[1024,256]{1,0:T(8,128)(2,1)S(1)} %bitcast.5, bf16[256,256]{1,0:T(8,128)(2,1)S(1)} %copy-done.5, bf16[256,512]{1,0:T(8,128)(2,1)S(1)} %copy-done.4, bf16[256,256]{1,0:T(8,128)(2,1)S(1)} %copy-done.6), custom_call_target="tpu_custom_call" | custom-call | tf_op jit(solution)/shard_map/row_attention/pallas_call | solution.py:118
  29.3 0.0 copy-start.2
  29.3 0.0 copy-start.3
  29.4 0.0 copy-start.7
  29.4 0.0 copy-start.8
  29.4 30.5 %all_to_all.16 = bf16[256,8,128]{2,1,0:T(8,128)(2,1)S(1)} all-to-all(bf16[256,8,128]{2,1,0:T(8,128)(2,1)S(1)} %bitcast.6), channel_id=1, replica_groups=mesh['lon'=16,'block'=8,'half'=2] {'lon','half','block'}, dimensions={0} | all-to-all | bytes 1048576 | tf_op jit(solution)/shard_map/all_to_all | solution.py:464
  59.9 4.9 %column_attention.1 = bf16[16,232,128]{2,1,0:T(8,128)(2,1)S(1)} custom-call(bf16[2048,128]{1,0:T(8,128)(2,1)S(1)} %bitcast.4, bf16[256,256]{1,0:T(8,128)(2,1)S(1)} %copy-done.7, bf16[256,512]{1,0:T(8,128)(2,1)S(1)} %copy-done.2, bf16[256,256]{1,0:T(8,128)(2,1)S(1)} %copy-done.8, bf16[512,224]{1,0:T(8,128)(2,1)S(1)} %copy-done.3), custom_call_target="tpu_custom_call" | custom-call | tf_op jit(solution)/shard_map/column_attention/pallas_call | solution.py:167
  64.7 25.9 %all_to_all.17.own_ref = bf16[16,232,128]{2,1,0:T(8,128)(2,1)S(1)} all-to-all(bf16[16,232,128]{2,1,0:T(8,128)(2,1)S(1)} %column_attention.1), channel_id=1, replica_groups=mesh['lon'=16,'block'=8,'half'=2] {'half','block'}, dimensions={0} | all-to-all | bytes 1900544 | tf_op jit(solution)/shard_map/all_to_all | solution.py:469
  90.7 2.8 %collective-permute-start.1 = (bf16[4,232,128]{2,1,0:T(8,128)(2,1)S(1)}, bf16[4,232,128]{2,1,0:T(8,128)(2,1)S(1)}, u32[]{:S(2)}, u32[]{:S(2)}) collective-permute-start(bf16[4,232,128]{2,1,0:T(8,128)(2,1)S(1)} %get-tuple-element.17), channel_id=1, source_target_pairs={{16,0},{32,16},{48,32},{64,48},{80,64},{96,80},{112,96},{128,112},... | collective-permute-start | bytes 712712 | tf_op jit(solution)/shard_map/ppermute | solution.py:472
  93.5 3.2 %collective-permute-start = (bf16[4,232,128]{2,1,0:T(8,128)(2,1)S(1)}, bf16[4,232,128]{2,1,0:T(8,128)(2,1)S(1)}, u32[]{:S(2)}, u32[]{:S(2)}) collective-permute-start(bf16[4,232,128]{2,1,0:T(8,128)(2,1)S(1)} %get-tuple-element.18), channel_id=1, source_target_pairs={{0,16},{16,32},{32,48},{48,64},{64,80},{80,96},{96,112},{112,128},... | collective-permute-start | bytes 712712 | tf_op jit(solution)/shard_map/ppermute | solution.py:471
  96.6 7.1 %inner_levels.1 = (bf16[3,58,16,128]{3,2,1,0:T(8,128)(2,1)S(1)}, bf16[44,56,128]{2,1,0:T(8,128)(2,1)S(1)}, bf16[28,32,128]{2,1,0:T(8,128)(2,1)S(1)}) custom-call(bf16[16,232,128]{2,1,0:T(8,128)(2,1)S(1)} %all_to_all.17.own_ref, f32[9,4,256]{2,1,0:T(4,128)S(1)} %bitcast.7), custom_call_target="tpu_custom_call" | custom-call | flops 60000000 | bytes 8000000 | tf_op jit(solution)/shard_map/inner_levels/pallas_call | solution.py:300
  103.8 0.0 copy-start
  103.8 0.0 copy-start.1
  103.8 4.4 %outer_levels.1 = (bf16[14,64,128]{2,1,0:T(8,128)(2,1)S(1)}, bf16[7,64,128]{2,1,0:T(8,128)(2,1)S(1)}, bf16[7,64,128]{2,1,0:T(8,128)(2,1)S(1)}) custom-call(bf16[4,232,128]{2,1,0:T(8,128)(2,1)S(1)} %collective-permute-done.left_ref, bf16[4,232,128]{2,1,0:T(8,128)(2,1)S(1)} %collective-permute-done.1.right_ref, ...), custom_call_target="tpu_custom_call" | custom-call | flops 40000000 | bytes 4000000 | tf_op jit(solution)/shard_map/outer_levels/pallas_call | solution.py:384
  108.2 0.3 collective-permute-start.3
  108.5 1.3 %collective-permute-start.2 = (bf16[7,64,128]{2,1,0:T(8,128)(2,1)S(1)}, bf16[7,64,128]{2,1,0:T(8,128)(2,1)S(1)}, u32[]{:S(2)}, u32[]{:S(2)}) collective-permute-start(bf16[7,64,128]{2,1,0:T(8,128)(2,1)S(1)} %get-tuple-element.15), channel_id=1, source_target_pairs={{0,1},{1,0},{2,3},{3,2},{4,5},{5,4},{6,7},{7,6},{8,9},{9,8},{10,11... | collective-permute-start | bytes 344072 | tf_op jit(solution)/shard_map/ppermute | solution.py:477
  109.7 2.6 %collective-permute-done.3.got_ref = bf16[7,64,128]{2,1,0:T(8,128)(2,1)S(1)} collective-permute-done((bf16[7,64,128]{2,1,0:T(8,128)(2,1)S(1)}, bf16[7,64,128]{2,1,0:T(8,128)(2,1)S(1)}, u32[]{:S(2)}, u32[]{:S(2)}) %collective-permute-start.3) | collective-permute-done | bytes 114720 | tf_op jit(solution)/shard_map/ppermute | solution.py:477
  112.3 2.1 %feed_forward.2.refs_0_ = bf16[14,64,256]{2,1,0:T(8,128)(2,1)} custom-call(bf16[14,64,128]{2,1,0:T(8,128)(2,1)S(1)} %get-tuple-element.14.keep_ref, bf16[7,64,128]{2,1,0:T(8,128)(2,1)S(1)} %collective-permute-done.3.got_ref, bf16[256,2048]{1,0:T(8,128)(2,1)S(1)} %copy-done, bf16[1024,256]{1,0:T(8,128)(2,1)S(1)} %copy-done.1), custom_call_target="tpu_custom_call" | custom-call | flops 700000000 | bytes 2000000 | tf_op jit(solution)/shard_map/feed_forward/pallas_call | solution.py:417
  114.4 2.1 %feed_forward.3 = bf16[14,64,256]{2,1,0:T(8,128)(2,1)} custom-call(bf16[14,64,128]{2,1,0:T(8,128)(2,1)S(1)} %get-tuple-element.14.keep_ref, bf16[7,64,128]{2,1,0:T(8,128)(2,1)S(1)} %collective-permute-done.2.got_ref, bf16[256,2048]{1,0:T(8,128)(2,1)S(1)} %copy-done, bf16[1024,256]{1,0:T(8,128)(2,1)S(1)} %copy-done.1, ...), custom_call_target="tpu_custom_call", output_to_operand_aliasing={{}: (4, {})} | custom-call | flops 700000000 | bytes 2000000 | tf_op jit(solution)/shard_map/feed_forward/pallas_call | solution.py:417
  (15 shorter events, 0.1 us)
Async XLA Ops:
  1.1 17.7 %copy-start.4 = (bf16[256,512]{1,0:T(8,128)(2,1)S(1)}, bf16[256,512]{1,0:T(8,128)(2,1)}, u32[]{:S(2)}) copy-start(bf16[256,512]{1,0:T(8,128)(2,1)} %wkv_ref.2) | copy-start | bytes 786436
  1.1 17.7 %copy-start.5 = (bf16[256,256]{1,0:T(8,128)(2,1)S(1)}, bf16[256,256]{1,0:T(8,128)(2,1)}, u32[]{:S(2)}) copy-start(bf16[256,256]{1,0:T(8,128)(2,1)} %wq_ref.2) | copy-start | bytes 393220
  1.1 17.7 %copy-start.6 = (bf16[256,256]{1,0:T(8,128)(2,1)S(1)}, bf16[256,256]{1,0:T(8,128)(2,1)}, u32[]{:S(2)}) copy-start(bf16[256,256]{1,0:T(8,128)(2,1)} %wo_ref.2) | copy-start | bytes 393220
  29.3 30.5 %copy-start.2 = (bf16[256,512]{1,0:T(8,128)(2,1)S(1)}, bf16[256,512]{1,0:T(8,128)(2,1)}, u32[]{:S(2)}) copy-start(bf16[256,512]{1,0:T(8,128)(2,1)} %wkv_ref.3) | copy-start | bytes 786436
  29.3 30.5 %copy-start.3 = (bf16[512,224]{1,0:T(8,128)(2,1)S(1)}, bf16[512,224]{1,0:T(8,128)(2,1)}, u32[]{:S(2)}) copy-start(bf16[512,224]{1,0:T(8,128)(2,1)} %constant.5.clone.sel_ref) | copy-start | bytes 688132
  29.4 30.5 %copy-start.7 = (bf16[256,256]{1,0:T(8,128)(2,1)S(1)}, bf16[256,256]{1,0:T(8,128)(2,1)}, u32[]{:S(2)}) copy-start(bf16[256,256]{1,0:T(8,128)(2,1)} %wq_ref.3) | copy-start | bytes 393220
  29.4 30.5 %copy-start.8 = (bf16[256,256]{1,0:T(8,128)(2,1)S(1)}, bf16[256,256]{1,0:T(8,128)(2,1)}, u32[]{:S(2)}) copy-start(bf16[256,256]{1,0:T(8,128)(2,1)} %wo_ref.3) | copy-start | bytes 393220
  90.6 6.0 %copy-start.9 = (f32[4,9,256]{2,0,1:T(4,128)S(1)}, f32[4,9,256]{2,0,1:T(4,128)}, u32[]{:S(2)}) copy-start(f32[4,9,256]{2,0,1:T(4,128)} %param.18) | copy-start | bytes 110596
  90.7 13.1 %collective-permute-start.1 = (bf16[4,232,128]{2,1,0:T(8,128)(2,1)S(1)}, bf16[4,232,128]{2,1,0:T(8,128)(2,1)S(1)}, u32[]{:S(2)}, u32[]{:S(2)}) collective-permute-start(bf16[4,232,128]{2,1,0:T(8,128)(2,1)S(1)} %get-tuple-element.17), channel_id=1, source_target_pairs={{16,0},{32,16},{48,32},{64,48},{80,64},{96,80},{112,96},{128,112},... | collective-permute-start | bytes 712712 | tf_op jit(solution)/shard_map/ppermute | solution.py:472
  93.5 10.3 %collective-permute-start = (bf16[4,232,128]{2,1,0:T(8,128)(2,1)S(1)}, bf16[4,232,128]{2,1,0:T(8,128)(2,1)S(1)}, u32[]{:S(2)}, u32[]{:S(2)}) collective-permute-start(bf16[4,232,128]{2,1,0:T(8,128)(2,1)S(1)} %get-tuple-element.18), channel_id=1, source_target_pairs={{0,16},{16,32},{32,48},{48,64},{64,80},{80,96},{96,112},{112,128},... | collective-permute-start | bytes 712712 | tf_op jit(solution)/shard_map/ppermute | solution.py:471
  103.8 8.5 %copy-start = (bf16[256,2048]{1,0:T(8,128)(2,1)S(1)}, bf16[256,2048]{1,0:T(8,128)(2,1)}, u32[]{:S(2)}) copy-start(bf16[256,2048]{1,0:T(8,128)(2,1)} %gu_ref.3) | copy-start | bytes 3145732
  103.8 8.5 %copy-start.1 = (bf16[1024,256]{1,0:T(8,128)(2,1)S(1)}, bf16[1024,256]{1,0:T(8,128)(2,1)}, u32[]{:S(2)}) copy-start(bf16[1024,256]{1,0:T(8,128)(2,1)} %down_ref.3) | copy-start | bytes 1572868
  108.2 4.1 %collective-permute-start.3 = (bf16[7,64,128]{2,1,0:T(8,128)(2,1)S(1)}, bf16[7,64,128]{2,1,0:T(8,128)(2,1)S(1)}, u32[]{:S(2)}, u32[]{:S(2)}) collective-permute-start(bf16[7,64,128]{2,1,0:T(8,128)(2,1)S(1)} %get-tuple-element.16), channel_id=1, source_target_pairs={{0,1},{1,0},{2,3},{3,2},{4,5},{5,4},{6,7},{7,6},{8,9},{9,8},{10,11... | collective-permute-start | bytes 344072 | tf_op jit(solution)/shard_map/ppermute | solution.py:477
  108.5 5.9 %collective-permute-start.2 = (bf16[7,64,128]{2,1,0:T(8,128)(2,1)S(1)}, bf16[7,64,128]{2,1,0:T(8,128)(2,1)S(1)}, u32[]{:S(2)}, u32[]{:S(2)}) collective-permute-start(bf16[7,64,128]{2,1,0:T(8,128)(2,1)S(1)} %get-tuple-element.15), channel_id=1, source_target_pairs={{0,1},{1,0},{2,3},{3,2},{4,5},{5,4},{6,7},{7,6},{8,9},{9,8},{10,11... | collective-permute-start | bytes 344072 | tf_op jit(solution)/shard_map/ppermute | solution.py:477

commit v7 on v6

--- a/solution.py
+++ b/solution.py
@@ -206,7 +206,7 @@
         lines.append(terms[0] + terms[1] + terms[2])
     total = lines[0] + lines[1] + lines[2]
     part = ROOT_HALF * total
-    return (cell(1, 1) + part + part * lax.erf(total)).astype(BF)
+    return (cell(1, 1) + (part + part * lax.erf(total))).astype(BF)
 
 
 def spread(part, buf, width, lon, rows):
@@ -393,8 +393,7 @@
     )(left, right, edge, mid, done, taps)
 
 
-def feed_kernel(part, keep_ref, got_ref, gu_ref, down_ref, *refs):
-    o_ref, o_s, sem = refs[-3:]
+def feed(part, keep_ref, got_ref, gu_ref, down_ref):
     rows, cols, _ = got_ref.shape
     half = lax.axis_index("half")
     keep = keep_ref[part * rows : part * rows + rows].reshape(rows * cols, 128)
@@ -405,22 +404,34 @@
     gate, up = both[:, :units], both[:, units:]
     hidden = (gate / (1.0 + jnp.exp(-gate)) * up).astype(BF)
     out = (state + mm(hidden, down_ref[...])).astype(BF)
-    o_s[...] = out.reshape(rows, cols, 256)
-    copy = pltpu.make_async_copy(o_s, o_ref.at[pl.ds(part * rows, rows)], sem)
-    copy.start()
-    copy.wait()
-
-
-def feed_forward(part, keep, got, gate_up, down, before=None):
-    anywhere = pl.BlockSpec(memory_space=pl.ANY)
+    return out.reshape(rows, cols, 256)
+
+
+def first_kernel(keep_ref, got_ref, gu_ref, down_ref, o_ref):
+    o_ref[...] = feed(0, keep_ref, got_ref, gu_ref, down_ref)
+
+
+def second_kernel(keep_ref, got_ref, gu_ref, down_ref, before_ref, o_ref, o_s, sems):
+    rows = got_ref.shape[0]
+    first = pltpu.make_async_copy(before_ref, o_ref.at[pl.ds(0, rows)], sems.at[0])
+    first.start()
+    o_s[...] = feed(1, keep_ref, got_ref, gu_ref, down_ref)
+    second = pltpu.make_async_copy(o_s, o_ref.at[pl.ds(rows, rows)], sems.at[1])
+    second.start()
+    first.wait()
+    second.wait()
+
+
+def feed_forward(keep, got, gate_up, down, before=None):
+    shape = got.shape[:2] + (256,)
     more = [] if before is None else [before]
+    last = bool(more)
     return pl.pallas_call(
-        functools.partial(feed_kernel, part),
-        out_shape=jax.ShapeDtypeStruct(keep.shape[:2] + (256,), BF),
-        in_specs=[VMEM] * 4 + [anywhere] * len(more),
-        out_specs=anywhere,
-        scratch_shapes=[pltpu.VMEM(got.shape[:2] + (256,), BF), pltpu.SemaphoreType.DMA],
-        input_output_aliases={4: 0} if more else {},
+        second_kernel if last else first_kernel,
+        out_shape=jax.ShapeDtypeStruct(keep.shape[:2] + (256,) if last else shape, BF),
+        in_specs=[VMEM] * (4 + len(more)),
+        out_specs=pl.BlockSpec(memory_space=pl.ANY) if last else VMEM,
+        scratch_shapes=[pltpu.VMEM(shape, BF), pltpu.SemaphoreType.DMA((2,))] if last else [],
         compiler_params=pltpu.CompilerParams(vmem_limit_bytes=LIMIT),
         cost_estimate=pl.CostEstimate(flops=700000000, bytes_accessed=2000000, transcendentals=500000),
         name="feed_forward",
@@ -475,8 +486,8 @@
     keep, near, far = outer_levels(left, right, edge, mid, done, taps, rows * m, rows, cols)
     swap = [(0, 1), (1, 0)]
     got = [lax.ppermute(part, "half", swap) for part in (near, far)]
-    out = feed_forward(0, keep, got[0], gate_up, down_proj)
-    return feed_forward(1, keep, got[1], gate_up, down_proj, out)
+    out = feed_forward(keep, got[0], gate_up, down_proj)
+    return feed_forward(keep, got[1], gate_up, down_proj, out)
 
 
 def solution(mesh):

time: 118 us -> 118 us (level)
  transfers between devices with their start and end apart: 4 -> 4, of which waited for: 1 -> 1; matrix products, arithmetic and copies ran while one was open for 0% -> 0% of each run, Pallas kernels for 8% -> 7%
where the time goes in v7:
time: 118 us; the launch traced here: 116 us
  blocking collectives  74 us (63%)
  Pallas kernels  30.5 us (26%)
  starting transfers between devices  7.52 us (6%)
  waiting for transfers between devices  2.59 us (2%)
    all_to_all x1, blocking collectives, on_device(): lax.all_to_all(after_rows.reshape(n * m, 2 * lons, 128), ('lon',) + lat,...  30.5 us
    all_to_all x1, blocking collectives, on_device(): own = lax.all_to_all(sent, lat, 0, 0, tiled=True)  25.9 us
    all_to_all x1, blocking collectives, on_device(): lax.all_to_all(padded, 'lon', 0, 0, tiled=True).reshape(n * cols, width)  17.7 us
    pallas_call x1, Pallas kernels, row_attention(): pl.pallas_call(functools.partial(row_kernel, qb), out_shape=jax.ShapeDtyp...  10.5 us
    pallas_call x1, Pallas kernels, inner_levels(): pl.pallas_call(functools.partial(inner_kernel, lats, rows), out_shape=(ja...  7.16 us
    pallas_call x1, Pallas kernels, column_attention(): pl.pallas_call(functools.partial(column_kernel, lons, span, unroll), out_...  4.86 us
    pallas_call x1, Pallas kernels, outer_levels(): pl.pallas_call(functools.partial(outer_kernel, lats), out_shape=shapes, i...  4.42 us
    pallas_call x2, Pallas kernels, feed_forward(): pl.pallas_call(second_kernel if last else first_kernel, out_shape=jax.Sha...  3.47 us
  transfers between devices with their start and end apart: 4, of which 1 were waited for; matrix products, arithmetic and copies ran while one was open for 0% of the time, Pallas kernels for 7%

profile of v7, /device:TPU:7, one launch (start us, length us, event | category | flops | bytes accessed | tf_op | source)
XLA Modules:
  0.0 116.1 jit_solution(13038036193345505207)
XLA Ops:
  0.0 1.1 pad.4
  1.1 0.0 copy-start.4
  1.1 0.0 copy-start.5
  1.1 0.0 copy-start.6
  1.1 17.7 %all_to_all.15 = bf16[16,64,256]{2,1,0:T(8,128)(2,1)S(1)} all-to-all(bf16[16,64,256]{2,1,0:T(8,128)(2,1)S(1)} %pad.4), channel_id=1, replica_groups=mesh['lon'=16,'block'=8,'half'=2] {'lon'}, dimensions={0} | all-to-all | bytes 1048576 | tf_op jit(solution)/shard_map/all_to_all | solution.py:473
  18.8 10.5 %row_attention.1 = bf16[2048,128]{1,0:T(8,128)(2,1)S(1)} custom-call(bf16[1024,256]{1,0:T(8,128)(2,1)S(1)} %bitcast.5, bf16[256,256]{1,0:T(8,128)(2,1)S(1)} %copy-done.5, bf16[256,512]{1,0:T(8,128)(2,1)S(1)} %copy-done.4, bf16[256,256]{1,0:T(8,128)(2,1)S(1)} %copy-done.6), custom_call_target="tpu_custom_call" | custom-call | tf_op jit(solution)/shard_map/row_attention/pallas_call | solution.py:118
  29.3 0.0 copy-start.2
  29.3 0.0 copy-start.3
  29.4 0.0 copy-start.7
  29.4 0.0 copy-start.8
  29.4 30.5 %all_to_all.16 = bf16[256,8,128]{2,1,0:T(8,128)(2,1)S(1)} all-to-all(bf16[256,8,128]{2,1,0:T(8,128)(2,1)S(1)} %bitcast.6), channel_id=1, replica_groups=mesh['lon'=16,'block'=8,'half'=2] {'lon','half','block'}, dimensions={0} | all-to-all | bytes 1048576 | tf_op jit(solution)/shard_map/all_to_all | solution.py:475
  59.9 4.9 %column_attention.1 = bf16[16,232,128]{2,1,0:T(8,128)(2,1)S(1)} custom-call(bf16[2048,128]{1,0:T(8,128)(2,1)S(1)} %bitcast.4, bf16[256,256]{1,0:T(8,128)(2,1)S(1)} %copy-done.7, bf16[256,512]{1,0:T(8,128)(2,1)S(1)} %copy-done.2, bf16[256,256]{1,0:T(8,128)(2,1)S(1)} %copy-done.8, bf16[512,224]{1,0:T(8,128)(2,1)S(1)} %copy-done.3), custom_call_target="tpu_custom_call" | custom-call | tf_op jit(solution)/shard_map/column_attention/pallas_call | solution.py:167
  64.7 25.9 %all_to_all.17.own_ref = bf16[16,232,128]{2,1,0:T(8,128)(2,1)S(1)} all-to-all(bf16[16,232,128]{2,1,0:T(8,128)(2,1)S(1)} %column_attention.1), channel_id=1, replica_groups=mesh['lon'=16,'block'=8,'half'=2] {'half','block'}, dimensions={0} | all-to-all | bytes 1900544 | tf_op jit(solution)/shard_map/all_to_all | solution.py:480
  90.7 2.8 %collective-permute-start.1 = (bf16[4,232,128]{2,1,0:T(8,128)(2,1)S(1)}, bf16[4,232,128]{2,1,0:T(8,128)(2,1)S(1)}, u32[]{:S(2)}, u32[]{:S(2)}) collective-permute-start(bf16[4,232,128]{2,1,0:T(8,128)(2,1)S(1)} %get-tuple-element.17), channel_id=1, source_target_pairs={{16,0},{32,16},{48,32},{64,48},{80,64},{96,80},{112,96},{128,112},... | collective-permute-start | bytes 712712 | tf_op jit(solution)/shard_map/ppermute | solution.py:483
  93.5 3.2 %collective-permute-start = (bf16[4,232,128]{2,1,0:T(8,128)(2,1)S(1)}, bf16[4,232,128]{2,1,0:T(8,128)(2,1)S(1)}, u32[]{:S(2)}, u32[]{:S(2)}) collective-permute-start(bf16[4,232,128]{2,1,0:T(8,128)(2,1)S(1)} %get-tuple-element.18), channel_id=1, source_target_pairs={{0,16},{16,32},{32,48},{48,64},{64,80},{80,96},{96,112},{112,128},... | collective-permute-start | bytes 712712 | tf_op jit(solution)/shard_map/ppermute | solution.py:482
  96.6 7.2 %inner_levels.1 = (bf16[3,58,16,128]{3,2,1,0:T(8,128)(2,1)S(1)}, bf16[44,56,128]{2,1,0:T(8,128)(2,1)S(1)}, bf16[28,32,128]{2,1,0:T(8,128)(2,1)S(1)}) custom-call(bf16[16,232,128]{2,1,0:T(8,128)(2,1)S(1)} %all_to_all.17.own_ref, f32[9,4,256]{2,1,0:T(4,128)S(1)} %bitcast.7), custom_call_target="tpu_custom_call" | custom-call | flops 60000000 | bytes 8000000 | tf_op jit(solution)/shard_map/inner_levels/pallas_call | solution.py:300
  103.8 0.0 copy-start
  103.8 0.0 copy-start.1
  103.8 4.4 %outer_levels.1 = (bf16[14,64,128]{2,1,0:T(8,128)(2,1)S(1)}, bf16[7,64,128]{2,1,0:T(8,128)(2,1)S(1)}, bf16[7,64,128]{2,1,0:T(8,128)(2,1)S(1)}) custom-call(bf16[4,232,128]{2,1,0:T(8,128)(2,1)S(1)} %collective-permute-done.left_ref, bf16[4,232,128]{2,1,0:T(8,128)(2,1)S(1)} %collective-permute-done.1.right_ref, ...), custom_call_target="tpu_custom_call" | custom-call | flops 40000000 | bytes 4000000 | tf_op jit(solution)/shard_map/outer_levels/pallas_call | solution.py:384
  108.3 0.3 collective-permute-start.3
  108.6 1.3 %collective-permute-start.2 = (bf16[7,64,128]{2,1,0:T(8,128)(2,1)S(1)}, bf16[7,64,128]{2,1,0:T(8,128)(2,1)S(1)}, u32[]{:S(2)}, u32[]{:S(2)}) collective-permute-start(bf16[7,64,128]{2,1,0:T(8,128)(2,1)S(1)} %get-tuple-element.15), channel_id=1, source_target_pairs={{0,1},{1,0},{2,3},{3,2},{4,5},{5,4},{6,7},{7,6},{8,9},{9,8},{10,11... | collective-permute-start | bytes 344072 | tf_op jit(solution)/shard_map/ppermute | solution.py:488
  109.8 2.6 %collective-permute-done.3.got_ref = bf16[7,64,128]{2,1,0:T(8,128)(2,1)S(1)} collective-permute-done((bf16[7,64,128]{2,1,0:T(8,128)(2,1)S(1)}, bf16[7,64,128]{2,1,0:T(8,128)(2,1)S(1)}, u32[]{:S(2)}, u32[]{:S(2)}) %collective-permute-start.3) | collective-permute-done | bytes 114720 | tf_op jit(solution)/shard_map/ppermute | solution.py:488
  112.4 1.4 %feed_forward.2.before_ref = bf16[7,64,256]{2,1,0:T(8,128)(2,1)S(1)} custom-call(bf16[14,64,128]{2,1,0:T(8,128)(2,1)S(1)} %get-tuple-element.14.keep_ref, bf16[7,64,128]{2,1,0:T(8,128)(2,1)S(1)} %collective-permute-done.3.got_ref, bf16[256,2048]{1,0:T(8,128)(2,1)S(1)} %copy-done, bf16[1024,256]{1,0:T(8,128)(2,1)S(1)} %copy-done.1), custom_call_target="tpu_custom_call" | custom-call | flops 700000000 | bytes 2000000 | tf_op jit(solution)/shard_map/feed_forward/pallas_call | solution.py:429
  113.8 2.1 %feed_forward.3 = bf16[14,64,256]{2,1,0:T(8,128)(2,1)} custom-call(bf16[14,64,128]{2,1,0:T(8,128)(2,1)S(1)} %get-tuple-element.14.keep_ref, bf16[7,64,128]{2,1,0:T(8,128)(2,1)S(1)} %collective-permute-done.2.got_ref, bf16[256,2048]{1,0:T(8,128)(2,1)S(1)} %copy-done, bf16[1024,256]{1,0:T(8,128)(2,1)S(1)} %copy-done.1, ...), custom_call_target="tpu_custom_call" | custom-call | flops 700000000 | bytes 2000000 | tf_op jit(solution)/shard_map/feed_forward/pallas_call | solution.py:429
  (15 shorter events, 0.1 us)
Async XLA Ops:
  1.1 17.7 %copy-start.4 = (bf16[256,512]{1,0:T(8,128)(2,1)S(1)}, bf16[256,512]{1,0:T(8,128)(2,1)}, u32[]{:S(2)}) copy-start(bf16[256,512]{1,0:T(8,128)(2,1)} %wkv_ref.2) | copy-start | bytes 786436
  1.1 17.7 %copy-start.5 = (bf16[256,256]{1,0:T(8,128)(2,1)S(1)}, bf16[256,256]{1,0:T(8,128)(2,1)}, u32[]{:S(2)}) copy-start(bf16[256,256]{1,0:T(8,128)(2,1)} %wq_ref.2) | copy-start | bytes 393220
  1.1 17.7 %copy-start.6 = (bf16[256,256]{1,0:T(8,128)(2,1)S(1)}, bf16[256,256]{1,0:T(8,128)(2,1)}, u32[]{:S(2)}) copy-start(bf16[256,256]{1,0:T(8,128)(2,1)} %wo_ref.2) | copy-start | bytes 393220
  29.3 30.5 %copy-start.2 = (bf16[256,512]{1,0:T(8,128)(2,1)S(1)}, bf16[256,512]{1,0:T(8,128)(2,1)}, u32[]{:S(2)}) copy-start(bf16[256,512]{1,0:T(8,128)(2,1)} %wkv_ref.3) | copy-start | bytes 786436
  29.3 30.5 %copy-start.3 = (bf16[512,224]{1,0:T(8,128)(2,1)S(1)}, bf16[512,224]{1,0:T(8,128)(2,1)}, u32[]{:S(2)}) copy-start(bf16[512,224]{1,0:T(8,128)(2,1)} %constant.5.clone.sel_ref) | copy-start | bytes 688132
  29.4 30.5 %copy-start.7 = (bf16[256,256]{1,0:T(8,128)(2,1)S(1)}, bf16[256,256]{1,0:T(8,128)(2,1)}, u32[]{:S(2)}) copy-start(bf16[256,256]{1,0:T(8,128)(2,1)} %wq_ref.3) | copy-start | bytes 393220
  29.4 30.5 %copy-start.8 = (bf16[256,256]{1,0:T(8,128)(2,1)S(1)}, bf16[256,256]{1,0:T(8,128)(2,1)}, u32[]{:S(2)}) copy-start(bf16[256,256]{1,0:T(8,128)(2,1)} %wo_ref.3) | copy-start | bytes 393220
  90.6 6.0 %copy-start.9 = (f32[4,9,256]{2,0,1:T(4,128)S(1)}, f32[4,9,256]{2,0,1:T(4,128)}, u32[]{:S(2)}) copy-start(f32[4,9,256]{2,0,1:T(4,128)} %param.18) | copy-start | bytes 110596
  90.7 13.2 %collective-permute-start.1 = (bf16[4,232,128]{2,1,0:T(8,128)(2,1)S(1)}, bf16[4,232,128]{2,1,0:T(8,128)(2,1)S(1)}, u32[]{:S(2)}, u32[]{:S(2)}) collective-permute-start(bf16[4,232,128]{2,1,0:T(8,128)(2,1)S(1)} %get-tuple-element.17), channel_id=1, source_target_pairs={{16,0},{32,16},{48,32},{64,48},{80,64},{96,80},{112,96},{128,112},... | collective-permute-start | bytes 712712 | tf_op jit(solution)/shard_map/ppermute | solution.py:483
  93.5 10.3 %collective-permute-start = (bf16[4,232,128]{2,1,0:T(8,128)(2,1)S(1)}, bf16[4,232,128]{2,1,0:T(8,128)(2,1)S(1)}, u32[]{:S(2)}, u32[]{:S(2)}) collective-permute-start(bf16[4,232,128]{2,1,0:T(8,128)(2,1)S(1)} %get-tuple-element.18), channel_id=1, source_target_pairs={{0,16},{16,32},{32,48},{48,64},{64,80},{80,96},{96,112},{112,128},... | collective-permute-start | bytes 712712 | tf_op jit(solution)/shard_map/ppermute | solution.py:482
  103.8 8.6 %copy-start = (bf16[256,2048]{1,0:T(8,128)(2,1)S(1)}, bf16[256,2048]{1,0:T(8,128)(2,1)}, u32[]{:S(2)}) copy-start(bf16[256,2048]{1,0:T(8,128)(2,1)} %gu_ref.3) | copy-start | bytes 3145732
  103.8 8.6 %copy-start.1 = (bf16[1024,256]{1,0:T(8,128)(2,1)S(1)}, bf16[1024,256]{1,0:T(8,128)(2,1)}, u32[]{:S(2)}) copy-start(bf16[1024,256]{1,0:T(8,128)(2,1)} %down_ref.3) | copy-start | bytes 1572868
  108.3 4.1 %collective-permute-start.3 = (bf16[7,64,128]{2,1,0:T(8,128)(2,1)S(1)}, bf16[7,64,128]{2,1,0:T(8,128)(2,1)S(1)}, u32[]{:S(2)}, u32[]{:S(2)}) collective-permute-start(bf16[7,64,128]{2,1,0:T(8,128)(2,1)S(1)} %get-tuple-element.16), channel_id=1, source_target_pairs={{0,1},{1,0},{2,3},{3,2},{4,5},{5,4},{6,7},{7,6},{8,9},{9,8},{10,11... | collective-permute-start | bytes 344072 | tf_op jit(solution)/shard_map/ppermute | solution.py:488
  108.6 5.2 %collective-permute-start.2 = (bf16[7,64,128]{2,1,0:T(8,128)(2,1)S(1)}, bf16[7,64,128]{2,1,0:T(8,128)(2,1)S(1)}, u32[]{:S(2)}, u32[]{:S(2)}) collective-permute-start(bf16[7,64,128]{2,1,0:T(8,128)(2,1)S(1)} %get-tuple-element.15), channel_id=1, source_target_pairs={{0,1},{1,0},{2,3},{3,2},{4,5},{5,4},{6,7},{7,6},{8,9},{9,8},{10,11... | collective-permute-start | bytes 344072 | tf_op jit(solution)/shard_map/ppermute | solution.py:488
